TPU v7x, 32 devices: a whole 2x2x4 slice. The times are simulated.
32 devices in a mesh: gx: 2 (over core), gy: 4 (over z), gz: 4 (over y, x).
Axes of the slice: x: 2, y: 2, z: 4, core: 2. Of those that a mesh axis runs over, the one named last changes fastest.
Arguments:
- probe_vectors: float32 [32, 4, 32, 512], P(None, 'gx', 'gy', 'gz'), may hold values from -6 to 6
- layer_ids: int32 [4, 32, 512], P('gx', 'gy', 'gz'), may hold values from 0 to 15
- layer_kappa: float32 [16], replicated, may hold values from 0.1 to 10
- slot_order: int32 [8, 4], replicated, may hold values from 0 to 31, as said below
Outputs:
- factored: float32 [1024, 1024], P(('gx', 'gy'), 'gz')
Inputs may be any that keep to these rules, and one draw needn't show every extreme that they name: `slot_order`: the entries are an ordering of 0 to 31, and in each column the entries divided by 4, rounded down, are an ordering of 0 to 7.
All inputs are finite; a program needn't handle non-finite values.
Results may differ from a plain program's by a relative error of at most 0.00013.
Values sent between devices are 32-bit elements; how exact they have to be, the bound alone decides.
A program may use at most 128 MiB of HBM per device.

v0:
```python
import math

import jax
import jax.numpy as jnp
from jax import lax
from jax.sharding import PartitionSpec as P

PASSES = 4
PANEL = 256
NPAN = 2


upper_edge = 120.0
lower_edge = 24.0
coarse_shift = 1.0


def with_halo(block, sides, width):
    for axis, dim in sides:
        count = lax.axis_size(axis)
        forward = [(i, i + 1) for i in range(count - 1)]
        backward = [(target, source) for source, target in forward]
        low = lax.ppermute(
            lax.slice_in_dim(block, block.shape[dim] - width, None, axis=dim), axis, forward
        )
        high = lax.ppermute(lax.slice_in_dim(block, 0, width, axis=dim), axis, backward)
        block = jnp.concatenate([low, block, high], axis=dim)
    return block


def from_root(value, axis, source):
    kept = jnp.where(lax.axis_index(axis) == source, value, 0).astype(value.dtype)
    return lax.psum(kept, axis)


def cheb_factors(step_index):
    center = (upper_edge + lower_edge) / (upper_edge - lower_edge)
    growth = math.log(center + math.sqrt(center * center - 1.0))

    def chebval(degree):
        expo = math.exp(degree * growth)
        return 0.5 * (expo + 1.0 / expo)

    if step_index == 0:
        return (1.0 / chebval(1), 0.0)
    return (
        2.0 * chebval(step_index) / chebval(step_index + 1),
        chebval(step_index - 1) / chebval(step_index + 1),
    )


def face_weights(kappa_pad):
    center = kappa_pad[1:-1, 1:-1, 1:-1]
    x_plus = 0.5 * (center + kappa_pad[2:, 1:-1, 1:-1])
    x_minus = 0.5 * (center + kappa_pad[:-2, 1:-1, 1:-1])
    y_plus = 0.5 * (center + kappa_pad[1:-1, 2:, 1:-1])
    y_minus = 0.5 * (center + kappa_pad[1:-1, :-2, 1:-1])
    z_plus = 0.5 * (center + kappa_pad[1:-1, 1:-1, 2:])
    z_minus = 0.5 * (center + kappa_pad[1:-1, 1:-1, :-2])
    diagonal = x_plus + x_minus + y_plus + y_minus + z_plus + z_minus
    return ((x_plus, x_minus, y_plus, y_minus, z_plus, z_minus), diagonal)


def apply_operator(field_pad, weights, diagonal):
    x_plus, x_minus, y_plus, y_minus, z_plus, z_minus = weights
    interior = field_pad[..., 1:-1, 1:-1, 1:-1]
    beside = x_plus * field_pad[..., 2:, 1:-1, 1:-1] + x_minus * field_pad[..., :-2, 1:-1, 1:-1]
    beside = (
        beside + y_plus * field_pad[..., 1:-1, 2:, 1:-1] + y_minus * field_pad[..., 1:-1, :-2, 1:-1]
    )
    beside = (
        beside + z_plus * field_pad[..., 1:-1, 1:-1, 2:] + z_minus * field_pad[..., 1:-1, 1:-1, :-2]
    )
    return diagonal * interior - beside


def cheb_update(current, previous, applied, step_index):
    factor_one, factor_two = cheb_factors(step_index)
    shifted = (upper_edge + lower_edge) / (upper_edge - lower_edge) * current - 2.0 / (
        upper_edge - lower_edge
    ) * applied
    return factor_one * shifted - factor_two * previous


def face_block(own_face, weight_face, ghost_face, scaling):
    return -scaling * jnp.einsum(
        "kab,ab,lab->kl", own_face, weight_face, ghost_face, precision=lax.Precision.HIGHEST
    )


def table_lookup(table, row_wanted, col_wanted):
    row_ids = jnp.arange(table.shape[0], dtype=jnp.int32)
    col_ids = jnp.arange(table.shape[1], dtype=jnp.int32)
    hit = (row_wanted[..., None, None] == row_ids[:, None]) & (
        col_wanted[..., None, None] == col_ids[None, :]
    )
    return jnp.sum(jnp.where(hit, table, 0), axis=(-2, -1))


def on_device(probe_vectors, layer_ids, layer_kappa, slot_order):
    highest = lax.Precision.HIGHEST
    grid_x = lax.axis_size("gx")
    grid_y = lax.axis_size("gy")
    grid_z = lax.axis_size("gz")
    index_x = lax.axis_index("gx")
    index_y = lax.axis_index("gy")
    index_z = lax.axis_index("gz")
    vectors, extent_x, extent_y, extent_z = probe_vectors.shape
    layers = layer_kappa.shape[0]
    choose = layer_ids[None] == jnp.arange(layers, dtype=jnp.int32)[:, None, None, None]
    conductivity = jnp.sum(jnp.where(choose, layer_kappa[:, None, None, None], 0.0), axis=0)
    kappa_pad = with_halo(conductivity, (("gx", 0), ("gy", 1), ("gz", 2)), 1)
    weights, diagonal = face_weights(kappa_pad)
    current = probe_vectors
    previous = jnp.zeros_like(probe_vectors)
    for step_index in range(PASSES):
        padded = with_halo(current, (("gx", 1), ("gy", 2), ("gz", 3)), 1)
        applied = apply_operator(padded, weights, diagonal)
        current, previous = (cheb_update(current, previous, applied, step_index), current)
    ghosts = with_halo(current, (("gx", 1), ("gy", 2), ("gz", 3)), 1)
    local_image = apply_operator(
        jnp.pad(current, ((0, 0), (1, 1), (1, 1), (1, 1))), weights, diagonal
    )
    cell_count = extent_x * extent_y * extent_z
    scaling = 1.0 / math.sqrt(cell_count)
    flattened = current.reshape(vectors, cell_count)
    own_block = scaling * jnp.dot(
        flattened, local_image.reshape(vectors, cell_count).T, precision=highest
    )
    own_block = own_block + coarse_shift * jnp.eye(vectors, dtype=jnp.float32)
    x_plus, x_minus, y_plus, y_minus, z_plus, z_minus = weights
    blocks = jnp.stack(
        [
            own_block,
            face_block(current[:, 0], x_minus[0], ghosts[:, 0, 1:-1, 1:-1], scaling),
            face_block(current[:, -1], x_plus[-1], ghosts[:, -1, 1:-1, 1:-1], scaling),
            face_block(current[:, :, 0], y_minus[:, 0], ghosts[:, 1:-1, 0, 1:-1], scaling),
            face_block(current[:, :, -1], y_plus[:, -1], ghosts[:, 1:-1, -1, 1:-1], scaling),
            face_block(current[:, :, :, 0], z_minus[:, :, 0], ghosts[:, 1:-1, 1:-1, 0], scaling),
            face_block(current[:, :, :, -1], z_plus[:, :, -1], ghosts[:, 1:-1, 1:-1, -1], scaling),
        ]
    )
    rows_total = grid_x * grid_y
    row_index = index_x * grid_y + index_y
    row_ids = jnp.arange(rows_total, dtype=jnp.int32)
    group_of = slot_order // grid_z
    column_groups = lax.dynamic_index_in_dim(group_of, index_z, 1, keepdims=False)
    owner_source = jnp.sum(jnp.where(column_groups == row_index, row_ids, 0))
    piece = lax.all_gather(blocks[None], ("gx", "gy"), axis=0, tiled=True)
    anchor = jnp.arange(piece.shape[0], dtype=jnp.int32)
    wanted = (anchor == owner_source)[:, None, None, None]
    owned = jnp.sum(jnp.where(wanted, piece, 0.0), axis=0)
    sources = jnp.arange(grid_z, dtype=jnp.int32)
    source_rows = jnp.sum(jnp.where(group_of == row_index, row_ids[:, None], 0), axis=0)
    source_x = source_rows // grid_y
    source_y = source_rows % grid_y
    neighbour_rows = jnp.stack(
        [
            source_rows,
            source_rows - grid_y,
            source_rows + grid_y,
            source_rows - 1,
            source_rows + 1,
            source_rows,
            source_rows,
        ],
        axis=1,
    )
    neighbour_cols = jnp.stack(
        [sources, sources, sources, sources, sources, sources - 1, sources + 1], axis=1
    )
    always = jnp.ones((grid_z,), bool)
    usable = jnp.stack(
        [
            always,
            source_x > 0,
            source_x < grid_x - 1,
            source_y > 0,
            source_y < grid_y - 1,
            sources > 0,
            sources < grid_z - 1,
        ],
        axis=1,
    )
    targets = table_lookup(slot_order, neighbour_rows, neighbour_cols)
    own_slots = table_lookup(slot_order, source_rows, sources) - row_index * grid_z
    local_cols = targets - index_z * rows_total
    usable = usable & (local_cols >= 0) & (local_cols < rows_total)
    col_flat = jnp.where(usable, local_cols, rows_total).reshape(-1)
    row_flat = jnp.broadcast_to(own_slots[:, None], (grid_z, 7)).reshape(-1)
    empty_grid = jnp.zeros((grid_z, vectors, rows_total, vectors), jnp.float32)
    gathered = empty_grid.at[row_flat, :, col_flat, :].add(
        lax.all_gather(owned, "gz", axis=0, tiled=True), mode="drop"
    )
    coarse = gathered.reshape(grid_z * vectors, rows_total * vectors)
    rows_local = coarse.shape[0]
    cols_local = coarse.shape[1]
    panel_width = min(PANEL, rows_local, cols_local)
    global_rows = row_index * rows_local + jnp.arange(rows_local, dtype=jnp.int32)
    global_cols = index_z * cols_local + jnp.arange(cols_local, dtype=jnp.int32)
    offsets = jnp.arange(panel_width, dtype=jnp.int32)
    for panel_index in range(NPAN):
        panel_begin = panel_index * panel_width
        panel_end = panel_begin + panel_width
        row_root = panel_begin // rows_local
        col_root = panel_begin // cols_local
        row_start = panel_begin - row_root * rows_local
        col_start = panel_begin - col_root * cols_local
        column_piece = from_root(coarse[:, col_start : col_start + panel_width], "gz", col_root)
        row_piece, diagonal_piece = (
            from_root(coarse[row_start : row_start + panel_width, :], ("gx", "gy"), row_root),
            from_root(column_piece[row_start : row_start + panel_width, :], ("gx", "gy"), row_root),
        )
        factor = jnp.linalg.cholesky(diagonal_piece)
        row_factor = jax.scipy.linalg.solve_triangular(factor, column_piece.T, lower=True).T
        col_factor = jax.scipy.linalg.solve_triangular(factor, row_piece, lower=True).T
        row_factor = jnp.where(
            global_rows[:, None] >= panel_begin + offsets[None, :], row_factor, 0.0
        )
        updated = coarse - jnp.dot(row_factor, col_factor.T, precision=highest)
        trail_rows = global_rows >= panel_end
        trail_cols = global_cols >= panel_end
        panel_rows = (global_rows >= panel_begin) & (global_rows < panel_end)
        coarse = jnp.where(
            trail_rows[:, None] & trail_cols[None, :],
            updated,
            jnp.where(panel_rows[:, None] & trail_cols[None, :], 0.0, coarse),
        )
        old_columns = coarse[:, col_start : col_start + panel_width]
        new_columns = jnp.where(index_z == col_root, row_factor, old_columns)
        coarse = coarse.at[:, col_start : col_start + panel_width].set(new_columns)
    return coarse


def solution(mesh):
    in_specs = (P(None, "gx", "gy", "gz"), P("gx", "gy", "gz"), P(), P())
    out_specs = P(("gx", "gy"), "gz")
    return jax.shard_map(
        on_device, mesh=mesh, in_specs=in_specs, out_specs=out_specs, check_vma=False
    )
```

profile of v0, /device:TPU:0, one launch (start us, length us, event | category | flops | bytes accessed | tf_op | source)
XLA Modules:
  0.0 453.8 jit_solution(1122617816206309576)
XLA Ops:
  17.0 4.9 %collective-permute-start.3 = (f32[4,1,128]{2,1,0:T(1,128)S(1)}, f32[4,1,128]{2,1,0:T(1,128)S(1)}, u32[]{:S(2)}, u32[]{:S(2)}) collective-permute-start(f32[4,1,128]{2,1,0:T(1,128)S(1)} %get-tuple-element.83), channel_id=1, source_target_pairs={{0,4},{4,8},{8,12},{1,5},{5,9},{9,13},{2,6},{6,10},{10,14},{3,7},{... | collective-permute-start | bytes 6152 | tf_op jit(solution)/shard_map/ppermute | solution.py:23
  28.8 4.5 %collective-permute-start.5 = (f32[4,10,1]{2,0,1:T(4,128)S(1)}, f32[4,10,1]{2,0,1:T(4,128)S(1)}, u32[]{:S(2)}, u32[]{:S(2)}) collective-permute-start(f32[4,10,1]{2,0,1:T(4,128)S(1)} %get-tuple-element.81), channel_id=1, source_target_pairs={{0,1},{1,2},{2,3},{4,5},{5,6},{6,7},{8,9},{9,10},{10,11},{12,13},{... | collective-permute-start | bytes 488 | tf_op jit(solution)/shard_map/ppermute | solution.py:23
  36.4 4.5 %collective-permute-start.9 = (f32[32,4,1,128]{3,0,2,1:T(8,128)S(1)}, f32[32,4,1,128]{3,0,2,1:T(8,128)S(1)}, u32[]{:S(2)}, u32[]{:S(2)}) collective-permute-start(f32[32,4,1,128]{3,0,2,1:T(8,128)S(1)} %get-tuple-element.67), channel_id=1, source_target_pairs={{0,4},{4,8},{8,12},{1,5},{5,9},{9,13},{2,6},{6,10},{10,14},{3,7},{... | collective-permute-start | bytes 196616 | tf_op jit(solution)/shard_map/ppermute | solution.py:23
  45.1 4.9 %collective-permute-start.11 = (f32[32,4,10,1]{0,1,3,2:T(4,128)S(1)}, f32[32,4,10,1]{0,1,3,2:T(4,128)S(1)}, u32[]{:S(2)}, u32[]{:S(2)}) collective-permute-start(f32[32,4,10,1]{0,1,3,2:T(4,128)S(1)} %copy.184), channel_id=1, source_target_pairs={{0,1},{1,2},{2,3},{4,5},{5,6},{6,7},{8,9},{9,10},{10,11},{12,13},{... | collective-permute-start | bytes 15368 | tf_op jit(solution)/shard_map/ppermute | solution.py:23
  58.8 4.9 %collective-permute-start.15 = (f32[32,4,1,128]{3,0,2,1:T(8,128)S(1)}, f32[32,4,1,128]{3,0,2,1:T(8,128)S(1)}, u32[]{:S(2)}, u32[]{:S(2)}) collective-permute-start(f32[32,4,1,128]{3,0,2,1:T(8,128)S(1)} %get-tuple-element.65), channel_id=1, source_target_pairs={{0,4},{4,8},{8,12},{1,5},{5,9},{9,13},{2,6},{6,10},{10,14},{3,7},{... | collective-permute-start | bytes 196616 | tf_op jit(solution)/shard_map/ppermute | solution.py:23
  67.8 5.7 %collective-permute-start.17 = (f32[32,4,10,1]{0,1,3,2:T(4,128)S(1)}, f32[32,4,10,1]{0,1,3,2:T(4,128)S(1)}, u32[]{:S(2)}, u32[]{:S(2)}) collective-permute-start(f32[32,4,10,1]{0,1,3,2:T(4,128)S(1)} %copy.188), channel_id=1, source_target_pairs={{0,1},{1,2},{2,3},{4,5},{5,6},{6,7},{8,9},{9,10},{10,11},{12,13},{... | collective-permute-start | bytes 15368 | tf_op jit(solution)/shard_map/ppermute | solution.py:23
  82.8 5.0 %collective-permute-start.21 = (f32[32,4,1,128]{3,0,2,1:T(8,128)S(1)}, f32[32,4,1,128]{3,0,2,1:T(8,128)S(1)}, u32[]{:S(2)}, u32[]{:S(2)}) collective-permute-start(f32[32,4,1,128]{3,0,2,1:T(8,128)S(1)} %get-tuple-element.63), channel_id=1, source_target_pairs={{0,4},{4,8},{8,12},{1,5},{5,9},{9,13},{2,6},{6,10},{10,14},{3,7},{... | collective-permute-start | bytes 196616 | tf_op jit(solution)/shard_map/ppermute | solution.py:23
  91.9 5.7 %collective-permute-start.23 = (f32[32,4,10,1]{0,1,3,2:T(4,128)S(1)}, f32[32,4,10,1]{0,1,3,2:T(4,128)S(1)}, u32[]{:S(2)}, u32[]{:S(2)}) collective-permute-start(f32[32,4,10,1]{0,1,3,2:T(4,128)S(1)} %copy.193), channel_id=1, source_target_pairs={{0,1},{1,2},{2,3},{4,5},{5,6},{6,7},{8,9},{9,10},{10,11},{12,13},{... | collective-permute-start | bytes 15368 | tf_op jit(solution)/shard_map/ppermute | solution.py:23
  106.4 4.9 %collective-permute-start.27 = (f32[32,4,1,128]{3,0,2,1:T(8,128)S(1)}, f32[32,4,1,128]{3,0,2,1:T(8,128)S(1)}, u32[]{:S(2)}, u32[]{:S(2)}) collective-permute-start(f32[32,4,1,128]{3,0,2,1:T(8,128)S(1)} %get-tuple-element.61), channel_id=1, source_target_pairs={{0,4},{4,8},{8,12},{1,5},{5,9},{9,13},{2,6},{6,10},{10,14},{3,7},{... | collective-permute-start | bytes 196616 | tf_op jit(solution)/shard_map/ppermute | solution.py:23
  115.4 5.7 %collective-permute-start.29 = (f32[32,4,10,1]{0,1,3,2:T(4,128)S(1)}, f32[32,4,10,1]{0,1,3,2:T(4,128)S(1)}, u32[]{:S(2)}, u32[]{:S(2)}) collective-permute-start(f32[32,4,10,1]{0,1,3,2:T(4,128)S(1)} %copy.197), channel_id=1, source_target_pairs={{0,1},{1,2},{2,3},{4,5},{5,6},{6,7},{8,9},{9,10},{10,11},{12,13},{... | collective-permute-start | bytes 15368 | tf_op jit(solution)/shard_map/ppermute | solution.py:23
  127.9 4.3 collective-permute-start.32
  134.2 4.3 collective-permute-done.33
  139.1 5.1 %collective-permute-start.34 = (f32[32,4,10,1]{0,1,3,2:T(4,128)S(1)}, f32[32,4,10,1]{0,1,3,2:T(4,128)S(1)}, u32[]{:S(2)}, u32[]{:S(2)}) collective-permute-start(f32[32,4,10,1]{0,1,3,2:T(4,128)S(1)} %copy.199), channel_id=1, source_target_pairs={{0,1},{1,2},{2,3},{4,5},{5,6},{6,7},{8,9},{9,10},{10,11},{12,13},{... | collective-permute-start | bytes 15368 | tf_op jit(solution)/shard_map/ppermute | solution.py:23
  146.4 5.0 %collective-permute-done.35 = f32[32,4,10,1]{0,1,3,2:T(4,128)S(1)} collective-permute-done((f32[32,4,10,1]{0,1,3,2:T(4,128)S(1)}, f32[32,4,10,1]{0,1,3,2:T(4,128)S(1)}, u32[]{:S(2)}, u32[]{:S(2)}) %collective-permute-start.35) | collective-permute-done | bytes 5152 | tf_op jit(solution)/shard_map/ppermute | solution.py:26
  151.6 29.9 %all-gather = f32[56,32,32]{2,1,0:T(8,128)S(1)} all-gather(f32[7,32,32]{2,1,0:T(8,128)S(1)} %fusion.6), channel_id=2, replica_groups=mesh['gx'=2,'gy'=4,'gz'=4] {'gx','gy'}, dimensions={0}, use_global_device_ids=true | all-gather | bytes 258048 | tf_op jit(solution)/shard_map/all_gather | solution.py:149
  181.7 11.4 %all_gather.7 = f32[28,32,32]{2,1,0:T(8,128)S(1)} all-gather(f32[7,32,32]{2,1,0:T(8,128)S(1)} %select_reduce_fusion), channel_id=1, replica_groups=mesh['gx'=2,'gy'=4,'gz'=4] {'gz'}, dimensions={0}, use_global_device_ids=true | all-gather | bytes 143360 | tf_op jit(solution)/shard_map/all_gather | solution.py:193
  197.4 39.6 %all-reduce.8.cloned.1.call-done = f32[128,128]{0,1:T(8,128)} async-done(((f32[128,128]{0,1:T(8,128)}), f32[128,128]{0,1:T(8,128)}) %all-reduce.8.cloned.1.call-update) | async-done | bytes 65552 | tf_op jit(solution)/shard_map/psum | solution.py:33
  238.6 55.7 %all-reduce.14.cloned.1.call-done = (f32[128,128]{0,1:T(8,128)}, f32[128,256]{0,1:T(8,128)}) async-done(((f32[128,128]{0,1:T(8,128)}, f32[128,256]{0,1:T(8,128)}), (f32[128,128]{0,1:T(8,128)}, f32[128,256]{0,1:T(8,128)})) %all-reduce.14.cloned.1.call-update) | async-done | bytes 196624 | tf_op jit(solution)/shard_map/psum | solution.py:33
  296.1 11.7 %cholesky.44 = f32[128,128]{1,0:T(8,128)S(1)} custom-call(f32[128,128]{1,0:T(8,128)S(1)} %fusion.129), custom_call_target="Cholesky" | custom-call | tf_op jit(solution)/shard_map/jit(cholesky)/cholesky | solution.py:214
  309.1 9.8 %custom-call.12 = f32[1,128,128]{1,2,0:T(8,128)S(1)} custom-call(f32[1,128,128]{2,1,0:T(8,128)S(1)} %fusion.116), custom_call_target="InvertDiagBlocksLowerTriangular" | custom-call | tf_op jit(solution)/shard_map/jit(_solve_triangular)/triangular_solve | solution.py:215
  323.1 39.7 %all-reduce.10.cloned.1.call-done = f32[128,128]{0,1:T(8,128)} async-done(((f32[128,128]{0,1:T(8,128)}), f32[128,128]{0,1:T(8,128)}) %all-reduce.10.cloned.1.call-update) | async-done | bytes 65552 | tf_op jit(solution)/shard_map/psum | solution.py:33
  363.5 56.5 %all-reduce.12.cloned.1.call-done = (f32[128,128]{0,1:T(8,128)}, f32[128,256]{0,1:T(8,128)}) async-done(((f32[128,128]{0,1:T(8,128)}, f32[128,256]{0,1:T(8,128)}), (f32[128,128]{0,1:T(8,128)}, f32[128,256]{0,1:T(8,128)})) %all-reduce.12.cloned.1.call-update) | async-done | bytes 196624 | tf_op jit(solution)/shard_map/psum | solution.py:33
  421.7 11.7 %cholesky.55 = f32[128,128]{1,0:T(8,128)S(1)} custom-call(f32[128,128]{1,0:T(8,128)S(1)} %fusion.124), custom_call_target="Cholesky" | custom-call | tf_op jit(solution)/shard_map/jit(cholesky)/cholesky | solution.py:214
  434.8 9.8 %custom-call.14 = f32[1,128,128]{1,2,0:T(8,128)S(1)} custom-call(f32[1,128,128]{2,1,0:T(8,128)S(1)} %fusion.117), custom_call_target="InvertDiagBlocksLowerTriangular" | custom-call | tf_op jit(solution)/shard_map/jit(_solve_triangular)/triangular_solve | solution.py:215
  (211 shorter events, 94.3 us)
Async XLA Ops:
  6.5 230.4 %all-reduce.8.cloned.1.call-start = ((), (), s32[]{:S(2)}) async-start(), calls=%async_computation | async-start | bytes 131072 | tf_op jit(solution)/shard_map/psum | solution.py:33
  7.4 9.6 %collective-permute-start = (f32[1,8,128]{2,1,0:T(8,128)S(1)}, f32[1,8,128]{2,1,0:T(8,128)S(1)}, u32[]{:S(2)}, u32[]{:S(2)}) collective-permute-start(f32[1,8,128]{2,1,0:T(8,128)S(1)} %get-tuple-element.86), channel_id=1, source_target_pairs={{16,0},{17,1},{18,2},{19,3},{20,4},{21,5},{22,6},{23,7},{24,8},{25... | collective-permute-start | bytes 12296 | tf_op jit(solution)/shard_map/ppermute | solution.py:26
  8.7 8.3 %collective-permute-start.1 = (f32[1,8,128]{2,1,0:T(8,128)S(1)}, f32[1,8,128]{2,1,0:T(8,128)S(1)}, u32[]{:S(2)}, u32[]{:S(2)}) collective-permute-start(f32[1,8,128]{2,1,0:T(8,128)S(1)} %get-tuple-element.85), channel_id=1, source_target_pairs={{0,16},{1,17},{2,18},{3,19},{4,20},{5,21},{6,22},{7,23},{8,24},{9,... | collective-permute-start | bytes 12296 | tf_op jit(solution)/shard_map/ppermute | solution.py:23
  12.8 22.1 %collective-permute-start.7 = (f32[32,1,8,128]{3,0,2,1:T(8,128)S(1)}, f32[32,1,8,128]{3,0,2,1:T(8,128)S(1)}, u32[]{:S(2)}, u32[]{:S(2)}) collective-permute-start(f32[32,1,8,128]{3,0,2,1:T(8,128)S(1)} %get-tuple-element.78), channel_id=1, source_target_pairs={{0,16},{1,17},{2,18},{3,19},{4,20},{5,21},{6,22},{7,23},{8,24},{9,... | collective-permute-start | bytes 393224 | tf_op jit(solution)/shard_map/ppermute | solution.py:23
  14.1 21.0 %collective-permute-start.6 = (f32[32,1,8,128]{3,0,2,1:T(8,128)S(1)}, f32[32,1,8,128]{3,0,2,1:T(8,128)S(1)}, u32[]{:S(2)}, u32[]{:S(2)}) collective-permute-start(f32[32,1,8,128]{3,0,2,1:T(8,128)S(1)} %get-tuple-element.77), channel_id=1, source_target_pairs={{16,0},{17,1},{18,2},{19,3},{20,4},{21,5},{22,6},{23,7},{24,8},{25... | collective-permute-start | bytes 393224 | tf_op jit(solution)/shard_map/ppermute | solution.py:26
  17.0 6.7 %collective-permute-start.3 = (f32[4,1,128]{2,1,0:T(1,128)S(1)}, f32[4,1,128]{2,1,0:T(1,128)S(1)}, u32[]{:S(2)}, u32[]{:S(2)}) collective-permute-start(f32[4,1,128]{2,1,0:T(1,128)S(1)} %get-tuple-element.83), channel_id=1, source_target_pairs={{0,4},{4,8},{8,12},{1,5},{5,9},{9,13},{2,6},{6,10},{10,14},{3,7},{... | collective-permute-start | bytes 6152 | tf_op jit(solution)/shard_map/ppermute | solution.py:23
  43.5 6.6 %collective-permute-start.10 = (f32[32,4,10,1]{0,1,3,2:T(4,128)S(1)}, f32[32,4,10,1]{0,1,3,2:T(4,128)S(1)}, u32[]{:S(2)}, u32[]{:S(2)}) collective-permute-start(f32[32,4,10,1]{0,1,3,2:T(4,128)S(1)} %copy.182), channel_id=1, source_target_pairs={{1,0},{2,1},{3,2},{5,4},{6,5},{7,6},{9,8},{10,9},{11,10},{13,12},{... | collective-permute-start | bytes 15368 | tf_op jit(solution)/shard_map/ppermute | solution.py:26
  57.5 6.9 %collective-permute-start.14 = (f32[32,4,1,128]{3,0,2,1:T(8,128)S(1)}, f32[32,4,1,128]{3,0,2,1:T(8,128)S(1)}, u32[]{:S(2)}, u32[]{:S(2)}) collective-permute-start(f32[32,4,1,128]{3,0,2,1:T(8,128)S(1)} %get-tuple-element.66), channel_id=1, source_target_pairs={{4,0},{8,4},{12,8},{5,1},{9,5},{13,9},{6,2},{10,6},{14,10},{7,3},{... | collective-permute-start | bytes 196616 | tf_op jit(solution)/shard_map/ppermute | solution.py:26
  58.8 6.8 %collective-permute-start.15 = (f32[32,4,1,128]{3,0,2,1:T(8,128)S(1)}, f32[32,4,1,128]{3,0,2,1:T(8,128)S(1)}, u32[]{:S(2)}, u32[]{:S(2)}) collective-permute-start(f32[32,4,1,128]{3,0,2,1:T(8,128)S(1)} %get-tuple-element.65), channel_id=1, source_target_pairs={{0,4},{4,8},{8,12},{1,5},{5,9},{9,13},{2,6},{6,10},{10,14},{3,7},{... | collective-permute-start | bytes 196616 | tf_op jit(solution)/shard_map/ppermute | solution.py:23
  66.2 7.4 %collective-permute-start.16 = (f32[32,4,10,1]{0,1,3,2:T(4,128)S(1)}, f32[32,4,10,1]{0,1,3,2:T(4,128)S(1)}, u32[]{:S(2)}, u32[]{:S(2)}) collective-permute-start(f32[32,4,10,1]{0,1,3,2:T(4,128)S(1)} %copy.186), channel_id=1, source_target_pairs={{1,0},{2,1},{3,2},{5,4},{6,5},{7,6},{9,8},{10,9},{11,10},{13,12},{... | collective-permute-start | bytes 15368 | tf_op jit(solution)/shard_map/ppermute | solution.py:26
  67.8 7.2 %collective-permute-start.17 = (f32[32,4,10,1]{0,1,3,2:T(4,128)S(1)}, f32[32,4,10,1]{0,1,3,2:T(4,128)S(1)}, u32[]{:S(2)}, u32[]{:S(2)}) collective-permute-start(f32[32,4,10,1]{0,1,3,2:T(4,128)S(1)} %copy.188), channel_id=1, source_target_pairs={{0,1},{1,2},{2,3},{4,5},{5,6},{6,7},{8,9},{9,10},{10,11},{12,13},{... | collective-permute-start | bytes 15368 | tf_op jit(solution)/shard_map/ppermute | solution.py:23
  81.5 6.9 %collective-permute-start.20 = (f32[32,4,1,128]{3,0,2,1:T(8,128)S(1)}, f32[32,4,1,128]{3,0,2,1:T(8,128)S(1)}, u32[]{:S(2)}, u32[]{:S(2)}) collective-permute-start(f32[32,4,1,128]{3,0,2,1:T(8,128)S(1)} %get-tuple-element.64), channel_id=1, source_target_pairs={{4,0},{8,4},{12,8},{5,1},{9,5},{13,9},{6,2},{10,6},{14,10},{7,3},{... | collective-permute-start | bytes 196616 | tf_op jit(solution)/shard_map/ppermute | solution.py:26
  82.8 6.9 %collective-permute-start.21 = (f32[32,4,1,128]{3,0,2,1:T(8,128)S(1)}, f32[32,4,1,128]{3,0,2,1:T(8,128)S(1)}, u32[]{:S(2)}, u32[]{:S(2)}) collective-permute-start(f32[32,4,1,128]{3,0,2,1:T(8,128)S(1)} %get-tuple-element.63), channel_id=1, source_target_pairs={{0,4},{4,8},{8,12},{1,5},{5,9},{9,13},{2,6},{6,10},{10,14},{3,7},{... | collective-permute-start | bytes 196616 | tf_op jit(solution)/shard_map/ppermute | solution.py:23
  90.3 7.4 %collective-permute-start.22 = (f32[32,4,10,1]{0,1,3,2:T(4,128)S(1)}, f32[32,4,10,1]{0,1,3,2:T(4,128)S(1)}, u32[]{:S(2)}, u32[]{:S(2)}) collective-permute-start(f32[32,4,10,1]{0,1,3,2:T(4,128)S(1)} %copy.191), channel_id=1, source_target_pairs={{1,0},{2,1},{3,2},{5,4},{6,5},{7,6},{9,8},{10,9},{11,10},{13,12},{... | collective-permute-start | bytes 15368 | tf_op jit(solution)/shard_map/ppermute | solution.py:26
  91.9 7.2 %collective-permute-start.23 = (f32[32,4,10,1]{0,1,3,2:T(4,128)S(1)}, f32[32,4,10,1]{0,1,3,2:T(4,128)S(1)}, u32[]{:S(2)}, u32[]{:S(2)}) collective-permute-start(f32[32,4,10,1]{0,1,3,2:T(4,128)S(1)} %copy.193), channel_id=1, source_target_pairs={{0,1},{1,2},{2,3},{4,5},{5,6},{6,7},{8,9},{9,10},{10,11},{12,13},{... | collective-permute-start | bytes 15368 | tf_op jit(solution)/shard_map/ppermute | solution.py:23
  105.1 6.9 %collective-permute-start.26 = (f32[32,4,1,128]{3,0,2,1:T(8,128)S(1)}, f32[32,4,1,128]{3,0,2,1:T(8,128)S(1)}, u32[]{:S(2)}, u32[]{:S(2)}) collective-permute-start(f32[32,4,1,128]{3,0,2,1:T(8,128)S(1)} %get-tuple-element.62), channel_id=1, source_target_pairs={{4,0},{8,4},{12,8},{5,1},{9,5},{13,9},{6,2},{10,6},{14,10},{7,3},{... | collective-permute-start | bytes 196616 | tf_op jit(solution)/shard_map/ppermute | solution.py:26
  106.4 6.8 %collective-permute-start.27 = (f32[32,4,1,128]{3,0,2,1:T(8,128)S(1)}, f32[32,4,1,128]{3,0,2,1:T(8,128)S(1)}, u32[]{:S(2)}, u32[]{:S(2)}) collective-permute-start(f32[32,4,1,128]{3,0,2,1:T(8,128)S(1)} %get-tuple-element.61), channel_id=1, source_target_pairs={{0,4},{4,8},{8,12},{1,5},{5,9},{9,13},{2,6},{6,10},{10,14},{3,7},{... | collective-permute-start | bytes 196616 | tf_op jit(solution)/shard_map/ppermute | solution.py:23
  113.8 7.5 %collective-permute-start.28 = (f32[32,4,10,1]{0,1,3,2:T(4,128)S(1)}, f32[32,4,10,1]{0,1,3,2:T(4,128)S(1)}, u32[]{:S(2)}, u32[]{:S(2)}) collective-permute-start(f32[32,4,10,1]{0,1,3,2:T(4,128)S(1)} %copy.195), channel_id=1, source_target_pairs={{1,0},{2,1},{3,2},{5,4},{6,5},{7,6},{9,8},{10,9},{11,10},{13,12},{... | collective-permute-start | bytes 15368 | tf_op jit(solution)/shard_map/ppermute | solution.py:26
  115.4 7.2 %collective-permute-start.29 = (f32[32,4,10,1]{0,1,3,2:T(4,128)S(1)}, f32[32,4,10,1]{0,1,3,2:T(4,128)S(1)}, u32[]{:S(2)}, u32[]{:S(2)}) collective-permute-start(f32[32,4,10,1]{0,1,3,2:T(4,128)S(1)} %copy.197), channel_id=1, source_target_pairs={{0,1},{1,2},{2,3},{4,5},{5,6},{6,7},{8,9},{9,10},{10,11},{12,13},{... | collective-permute-start | bytes 15368 | tf_op jit(solution)/shard_map/ppermute | solution.py:23
  139.1 7.1 %collective-permute-start.34 = (f32[32,4,10,1]{0,1,3,2:T(4,128)S(1)}, f32[32,4,10,1]{0,1,3,2:T(4,128)S(1)}, u32[]{:S(2)}, u32[]{:S(2)}) collective-permute-start(f32[32,4,10,1]{0,1,3,2:T(4,128)S(1)} %copy.199), channel_id=1, source_target_pairs={{0,1},{1,2},{2,3},{4,5},{5,6},{6,7},{8,9},{9,10},{10,11},{12,13},{... | collective-permute-start | bytes 15368 | tf_op jit(solution)/shard_map/ppermute | solution.py:23
  144.5 6.9 %collective-permute-start.35 = (f32[32,4,10,1]{0,1,3,2:T(4,128)S(1)}, f32[32,4,10,1]{0,1,3,2:T(4,128)S(1)}, u32[]{:S(2)}, u32[]{:S(2)}) collective-permute-start(f32[32,4,10,1]{0,1,3,2:T(4,128)S(1)} %copy.201), channel_id=1, source_target_pairs={{1,0},{2,1},{3,2},{5,4},{6,5},{7,6},{9,8},{10,9},{11,10},{13,12},{... | collective-permute-start | bytes 15368 | tf_op jit(solution)/shard_map/ppermute | solution.py:26
  196.7 97.6 %all-reduce.14.cloned.1.call-start = ((), (), s32[]{:S(2)}) async-start(), calls=%async_computation.3 | async-start | bytes 393216 | tf_op jit(solution)/shard_map/psum | solution.py:33
  238.5 124.3 %all-reduce.10.cloned.1.call-start = ((), (), s32[]{:S(2)}) async-start(), calls=%async_computation.1 | async-start | bytes 131072 | tf_op jit(solution)/shard_map/psum | solution.py:33
  322.2 97.8 %all-reduce.12.cloned.1.call-start = ((), (), s32[]{:S(2)}) async-start(), calls=%async_computation.2 | async-start | bytes 393216 | tf_op jit(solution)/shard_map/psum | solution.py:33
  (20 other events, 285.8 us)
Sparse Core Ops, SparseCore 0:
  196.8 40.1 all-reduce.7
  239.5 54.7 all-reduce.13
  322.3 40.4 all-reduce.9
  365.2 54.7 all-reduce.11
where the time goes:
time: 455 us; the launch traced here: 454 us
  waiting for transfers between devices  220 us (48%)
  starting transfers between devices  98.7 us (22%)
  other arithmetic  61.5 us (14%)
  blocking collectives  41.3 us (9%)
  between operations  14.1 us (3%)
  local copies, waits for them, and re-layouts  12.6 us (3%)
  matrix products  5.55 us (1%)
    psum x4, waiting for transfers between devices, from_root(): return lax.psum(kept, axis)  191 us
    ppermute x18, starting transfers between devices, with_halo(): lax.ppermute(lax.slice_in_dim(block, block.shape[dim] - width, None, axis...  75.1 us
    all_gather x1, blocking collectives, on_device(): piece = lax.all_gather(blocks[None], ('gx', 'gy'), axis=0, tiled=True)  29.9 us
    another operation x6, other arithmetic, on_device(): factor = jnp.linalg.cholesky(diagonal_piece)  24.8 us
    ppermute x18, starting transfers between devices, with_halo(): lax.ppermute(lax.slice_in_dim(block, 0, width, axis=dim), axis, backward)  23.3 us
    another operation x4, other arithmetic, on_device(): jax.scipy.linalg.solve_triangular(factor, column_piece.T, lower=True)  20.9 us
    ppermute x18, waiting for transfers between devices, with_halo(): lax.ppermute(lax.slice_in_dim(block, 0, width, axis=dim), axis, backward)  15.5 us
    ppermute x18, waiting for transfers between devices, with_halo(): lax.ppermute(lax.slice_in_dim(block, block.shape[dim] - width, None, axis...  13 us
  transfers between devices with their start and end apart: 40, of which 23 were waited for; matrix products, arithmetic and copies ran while one was open for 3% of the time, Pallas kernels for 0%

commit v1 on v0

v1 whole, which is shorter than its diff:
```python
import functools
import math

import jax
import jax.numpy as jnp
from jax import lax
from jax.experimental import pallas as pl
from jax.experimental.pallas import tpu as pltpu
from jax.sharding import PartitionSpec as P

PASSES = 4
PANEL = 256
NPAN = 2
UPPER_EDGE = 120.0
LOWER_EDGE = 24.0
COARSE_SHIFT = 1.0
LANES = 128
MESH = pl.DeviceIdType.MESH
HIGHEST = lax.Precision.HIGHEST


def cheb_factors(step_index):
    center = (UPPER_EDGE + LOWER_EDGE) / (UPPER_EDGE - LOWER_EDGE)
    growth = math.log(center + math.sqrt(center * center - 1.0))

    def chebval(degree):
        expo = math.exp(degree * growth)
        return 0.5 * (expo + 1.0 / expo)

    if step_index == 0:
        return (1.0 / chebval(1), 0.0)
    return (
        2.0 * chebval(step_index) / chebval(step_index + 1),
        chebval(step_index - 1) / chebval(step_index + 1),
    )


def basis_kernel(
    counts, extents, vectors, layers,
    probe_ref, ids_ref, kappa_ref, out_ref,
    field, zsend, zrecv, weight, send_sem, recv_sem,
    line_send, line_recv, own_send, own_recv,
):
    nx, ny, nz = counts
    ex, ey, ez = extents
    groups = vectors // 8
    cells = ex * ey
    ix, iy, iz = lax.axis_index("gx"), lax.axis_index("gy"), lax.axis_index("gz")
    lines = (("gx", ix, nx), ("gy", iy, ny), ("gz", iz, nz))

    barrier = pltpu.get_barrier_semaphore()
    for axis, index, count in lines:
        for step in range(1, count):
            pl.semaphore_signal(
                barrier, inc=1, device_id={axis: lax.rem(index + step, count)}, device_id_type=MESH
            )

    lane = lax.broadcasted_iota(jnp.int32, (1, 8, ez), 2)
    zero_plane = jnp.zeros((groups + 1, 8, ez), jnp.float32)

    ids = ids_ref[...]
    kappa = jnp.zeros(ids.shape, jnp.float32)
    for layer in range(layers):
        kappa = jnp.where(ids == layer, kappa_ref[layer], kappa)
    for x in range(ex):
        for y in range(ey):
            k = x * ey + y
            field[0, x + 1, y + 1, 0:groups] = probe_ref[
                pl.ds(k, vectors, stride=cells), :
            ].reshape(groups, 8, ez)
            field[0, x + 1, y + 1, groups] = jnp.broadcast_to(kappa[k : k + 1, :], (8, ez))

    inside = (ix > 0, ix < nx - 1, iy > 0, iy < ny - 1, iz > 0, iz < nz - 1)

    def clear(side, phase):
        if side < 2:
            for y in range(ey):
                field[phase, 0 if side == 0 else ex + 1, y + 1] = zero_plane
        elif side < 4:
            for x in range(ex):
                field[phase, x + 1, 0 if side == 2 else ey + 1] = zero_plane
        else:
            zrecv[phase, side - 4] = zero_plane

    for side in range(6):
        @pl.when(jnp.logical_not(inside[side]))
        def _():
            for phase in range(PASSES + 1):
                clear(side, phase)

    def copy_of(phase, side):
        span = pl.ds(0, groups + 1 if phase == 0 else groups)
        axis, index, _ = lines[side // 2]
        low = side % 2 == 0
        target = index - 1 if low else index + 1
        if side < 2:
            src = field.at[phase, 1 if low else ex, pl.ds(1, ey), span]
            dst = field.at[phase, ex + 1 if low else 0, pl.ds(1, ey), span]
        elif side < 4:
            src = field.at[phase, pl.ds(1, ex), 1 if low else ey, span]
            dst = field.at[phase, pl.ds(1, ex), ey + 1 if low else 0, span]
        else:
            src = zsend.at[phase, 0 if low else 1, span]
            dst = zrecv.at[phase, 1 if low else 0, span]
        return pltpu.make_async_remote_copy(
            src_ref=src, dst_ref=dst,
            send_sem=send_sem.at[phase, side], recv_sem=recv_sem.at[phase, side],
            device_id={axis: target}, device_id_type=MESH,
        )

    def sides_of(phase):
        return range(6) if phase < PASSES else (0, 2, 4)

    def send(phase):
        span = groups + 1 if phase == 0 else groups
        for low in ((True, False) if phase < PASSES else (True,)):
            packed = jnp.zeros((span, 8, ez), jnp.float32)
            for x in range(ex):
                for y in range(ey):
                    k = x * ey + y
                    value = field[phase, x + 1, y + 1, 0:span]
                    shift = k if low else k + 1
                    if shift:
                        value = pltpu.roll(value, shift, 2)
                    packed = jnp.where(lane == k, value, packed)
            zsend[phase, 0 if low else 1, 0:span] = packed
        for side in sides_of(phase):
            @pl.when(inside[side])
            def _():
                copy_of(phase, side).start()

    def receive(phase):
        for side in sides_of(phase):
            @pl.when(inside[side ^ 1])
            def _():
                copy_of(phase, side).wait_recv()

    def z_neighbours(phase, k, value, part):
        span = value.shape[0]
        above = pltpu.roll(value, ez - 1, 2)
        ghost = zrecv[phase, 1, part : part + span]
        if (ez - 1 - k) % ez:
            ghost = pltpu.roll(ghost, ez - 1 - k, 2)
        above = jnp.where(lane == ez - 1, ghost, above)
        if phase == PASSES:
            return above, None
        below = pltpu.roll(value, 1, 2)
        ghost = zrecv[phase, 0, part : part + span]
        if k:
            ghost = pltpu.roll(ghost, ez - k, 2)
        return above, jnp.where(lane == 0, ghost, below)

    pl.semaphore_wait(barrier, sum(count - 1 for _, _, count in lines))

    for phase in range(PASSES):
        send(phase)
        receive(phase)
        if phase == 0:
            for x in range(1, ex + 1):
                for y in range(1, ey + 1):
                    k = (x - 1) * ey + y - 1
                    here = field[0, x, y, groups : groups + 1]
                    above, below = z_neighbours(0, k, here, groups)
                    beside = (
                        field[0, x + 1, y, groups : groups + 1], field[0, x - 1, y, groups : groups + 1],
                        field[0, x, y + 1, groups : groups + 1], field[0, x, y - 1, groups : groups + 1],
                        above, below,
                    )
                    total = None
                    for face in range(6):
                        value = 0.5 * (here + beside[face])
                        total = value if total is None else total + value
                        weight[face, k] = value[0]
                    weight[6, k] = total[0]
        factor_one, factor_two = cheb_factors(phase)
        shift = (UPPER_EDGE + LOWER_EDGE) / (UPPER_EDGE - LOWER_EDGE)
        slope = 2.0 / (UPPER_EDGE - LOWER_EDGE)
        for x in range(1, ex + 1):
            for y in range(1, ey + 1):
                k = (x - 1) * ey + y - 1
                here = field[phase, x, y, 0:groups]
                above, below = z_neighbours(phase, k, here, 0)
                beside = weight[0, k][None] * field[phase, x + 1, y, 0:groups]
                beside += weight[1, k][None] * field[phase, x - 1, y, 0:groups]
                beside += weight[2, k][None] * field[phase, x, y + 1, 0:groups]
                beside += weight[3, k][None] * field[phase, x, y - 1, 0:groups]
                beside += weight[4, k][None] * above + weight[5, k][None] * below
                applied = weight[6, k][None] * here - beside
                value = factor_one * (shift * here - slope * applied)
                if phase > 0:
                    value -= factor_two * field[phase - 1, x, y, 0:groups]
                field[phase + 1, x, y, 0:groups] = value

    send(PASSES)
    left, own = [], []
    for x in range(1, ex + 1):
        for y in range(1, ey + 1):
            k = (x - 1) * ey + y - 1
            here = field[PASSES, x, y, 0:groups]
            image = weight[6, k][None] * here
            if x < ex:
                image -= weight[0, k][None] * field[PASSES, x + 1, y, 0:groups]
            if x > 1:
                image -= weight[1, k][None] * field[PASSES, x - 1, y, 0:groups]
            if y < ey:
                image -= weight[2, k][None] * field[PASSES, x, y + 1, 0:groups]
            if y > 1:
                image -= weight[3, k][None] * field[PASSES, x, y - 1, 0:groups]
            above = jnp.where(lane == ez - 1, 0.0, pltpu.roll(here, ez - 1, 2))
            below = jnp.where(lane == 0, 0.0, pltpu.roll(here, 1, 2))
            image -= weight[4, k][None] * above + weight[5, k][None] * below
            left.append(here.reshape(vectors, ez))
            own.append(image.reshape(vectors, ez))
    receive(PASSES)
    right = []
    zeros = jnp.zeros((vectors, ez), jnp.float32)
    for x in range(1, ex + 1):
        for y in range(1, ey + 1):
            k = (x - 1) * ey + y - 1
            rows = [own[k], zeros, zeros]
            if x == ex:
                rows[1] = (-weight[0, k][None] * field[PASSES, x + 1, y, 0:groups]).reshape(vectors, ez)
            if y == ey:
                rows[2] = (-weight[2, k][None] * field[PASSES, x, y + 1, 0:groups]).reshape(vectors, ez)
            ghost = zrecv[PASSES, 1, 0:groups]
            if (ez - 1 - k) % ez:
                ghost = pltpu.roll(ghost, ez - 1 - k, 2)
            ghost = jnp.where(lane == ez - 1, -weight[4, k][None] * ghost, 0.0)
            rows.append(ghost.reshape(vectors, ez))
            right.append(jnp.concatenate(rows, axis=0))
    product = lax.dot_general(
        jnp.concatenate(left, axis=1), jnp.concatenate(right, axis=1),
        (((1,), (1,)), ((), ())), precision=HIGHEST, preferred_element_type=jnp.float32,
    ) * (1.0 / math.sqrt(cells * ez))
    row = lax.broadcasted_iota(jnp.int32, product.shape, 0)
    column = lax.broadcasted_iota(jnp.int32, product.shape, 1)
    out_ref[iz, ix, iy] = product + jnp.where(row == column, COARSE_SHIFT, 0.0)

    waits = []

    def spread(axis, index, count, ref_of, sends, recvs):
        copies = []
        for step in range(1, count):
            copy = pltpu.make_async_remote_copy(
                src_ref=ref_of(index), dst_ref=ref_of(index),
                send_sem=sends.at[step], recv_sem=recvs.at[step],
                device_id={axis: lax.rem(index + step, count)}, device_id_type=MESH,
            )
            copy.start()
            copies.append(copy)
        for step in range(1, count):
            source = ref_of(lax.rem(index + count - step, count))
            pltpu.make_async_remote_copy(
                src_ref=source, dst_ref=source,
                send_sem=sends.at[step], recv_sem=recvs.at[step],
                device_id={axis: lax.rem(index + step, count)}, device_id_type=MESH,
            ).wait_recv()
        waits.extend(copies)

    spread("gy", iy, ny, lambda i: out_ref.at[iz, ix, i], line_send.at[0], line_recv.at[0])
    spread("gz", iz, nz, lambda i: out_ref.at[i, ix], line_send.at[1], line_recv.at[1])
    spread("gx", ix, nx, lambda i: out_ref.at[:, i], line_send.at[2], line_recv.at[2])
    for copy in waits:
        copy.wait_send()
    for phase in range(PASSES + 1):
        for side in sides_of(phase):
            @pl.when(inside[side])
            def _():
                copy_of(phase, side).wait_send()


def factor_kernel(
    counts, vectors, width, rows_local, cols_local,
    slot_ref, blocks_ref, out_ref, place, panel, local, pivots,
):
    nx, ny, nz = counts
    ix, iy, iz = lax.axis_index("gx"), lax.axis_index("gy"), lax.axis_index("gz")
    rows_total = nx * ny
    row_block = (ix * ny + iy) * (rows_local // vectors)
    col_block = iz * (cols_local // vectors)
    wide = width // vectors
    per_tile = LANES // vectors

    def note(s, carry):
        place[slot_ref[s]] = s
        return carry

    lax.fori_loop(0, rows_total * nz, note, 0)
    panel[...] = jnp.zeros(panel.shape, jnp.float32)
    local[...] = jnp.zeros(local.shape, jnp.float32)
    lane = lax.broadcasted_iota(jnp.int32, (vectors, LANES), 1)

    def put(ref, row_at, col_at, value):
        rows = pl.ds(pl.multiple_of(row_at * vectors, vectors), vectors)
        cols = pl.ds(pl.multiple_of((col_at // per_tile) * LANES, LANES), LANES)
        ref[rows, cols] += pltpu.roll(value, (col_at % per_tile) * vectors, 1)

    def block_row(q, store):
        s = place[q]
        r, l = s // nz, s % nz
        i, j = r // ny, r % ny
        steps = ((ny, 0, i < nx - 1, i > 0), (1, 0, j < ny - 1, j > 0), (0, 1, l < nz - 1, l > 0))
        mine = blocks_ref[l, i, j]
        store(q, jnp.where(lane < vectors, mine, 0.0))
        for face, (dr, dl, up, down) in enumerate(steps):
            @pl.when(up)
            def _():
                value = pltpu.roll(mine, LANES - (face + 1) * vectors, 1)
                store(slot_ref[(r + dr) * nz + l + dl], jnp.where(lane < vectors, value, 0.0))

            @pl.when(down)
            def _():
                r2, l2 = r - dr, l - dl
                other = blocks_ref[l2, r2 // ny, r2 % ny]
                square = jnp.concatenate(
                    [other, jnp.zeros((LANES - vectors, LANES), jnp.float32)], axis=0
                )
                at = (face + 1) * vectors
                store(slot_ref[r2 * nz + l2], square.T[at : at + vectors, :])

    def top_row(q, carry):
        def store(c, value):
            pl.when(c < wide)(lambda: put(panel, q, c, value))
            pl.when((c >= col_block) & (c < col_block + cols_local // vectors))(
                lambda: put(panel, q, wide + c - col_block, value)
            )
            pl.when((c >= row_block) & (c < row_block + rows_local // vectors))(
                lambda: put(panel, q, wide + cols_local // vectors + c - row_block, value)
            )

        block_row(q, store)
        return carry

    def own_row(n, carry):
        def store(c, value):
            pl.when((c >= col_block) & (c < col_block + cols_local // vectors))(
                lambda: put(local, n, c - col_block, value)
            )

        block_row(row_block + n, store)
        return carry

    lax.fori_loop(0, wide, top_row, 0)
    lax.fori_loop(0, rows_local // vectors, own_row, 0)

    row8 = lax.broadcasted_iota(jnp.int32, (vectors, LANES), 0)

    def eliminate(b, carry):
        rows = pl.ds(pl.multiple_of(b * vectors, vectors), vectors)
        tile = pl.ds(pl.multiple_of((b // per_tile) * LANES, LANES), LANES)
        near = pltpu.roll(panel[rows, tile], (LANES - (b % per_tile) * vectors) % LANES, 1)
        body = panel[rows, :]
        pivot = jnp.ones((vectors, LANES), jnp.float32)
        inverse = jnp.ones((vectors, LANES), jnp.float32)
        for first in range(0, vectors, 8):
            columns = [
                jnp.broadcast_to(near[:, first + t : first + t + 1], (vectors, LANES)) for t in range(8)
            ]
            for t in range(8):
                j = first + t
                head = columns[t][j : j + 1, :]
                turn = 1.0 / head
                pivot = jnp.where(row8 == j, head, pivot)
                inverse = jnp.where(row8 == j, turn, inverse)
                factor = jnp.where(row8 > j, columns[t] * turn, 0.0)
                for u in range(t + 1, 8):
                    columns[u] = columns[u] - factor * columns[u][j : j + 1, :]
                near = near - factor * near[j : j + 1, :]
                spread = jnp.concatenate([factor] * (body.shape[1] // LANES), axis=1)
                body = body - spread * body[j : j + 1, :]
        panel[rows, :] = body
        pivots[rows, :] = pivot

        scaled = jnp.concatenate([inverse] * (width // LANES), axis=1) * body[:, :width]
        column = lax.broadcasted_iota(jnp.int32, scaled.shape, 1)
        scaled = jnp.where(column >= (b + 1) * vectors, scaled, 0.0)
        panel[...] -= jnp.dot(
            scaled.T, body, precision=HIGHEST, preferred_element_type=jnp.float32
        )
        return carry

    lax.fori_loop(0, wide, eliminate, 0)

    scale = lax.rsqrt(pivots[...])
    for tile in range(panel.shape[1] // LANES):
        if tile >= width // LANES:
            at = slice(tile * LANES, (tile + 1) * LANES)
            panel[:, at] = panel[:, at] * scale

    across = panel[:, width + cols_local :].T
    update = jnp.dot(
        across, panel[:, width : width + cols_local],
        precision=HIGHEST, preferred_element_type=jnp.float32,
    )
    row_ids = row_block * vectors + lax.broadcasted_iota(jnp.int32, (rows_local, LANES), 0)
    for tile in range(cols_local // LANES):
        at = slice(tile * LANES, (tile + 1) * LANES)
        start = iz * cols_local + tile * LANES
        col_ids = start + lax.broadcasted_iota(jnp.int32, (rows_local, LANES), 1)

        @pl.when(start < width)
        def _():
            part = panel[pl.ds(pl.multiple_of(start, LANES), LANES), width + cols_local :]
            out_ref[:, at] = jnp.where(col_ids <= row_ids, part.T, 0.0)

        @pl.when(start >= width)
        def _():
            rest = local[:, at] - update[:, at]
            out_ref[:, at] = jnp.where(row_ids >= width, rest, 0.0)


def on_device(probe_vectors, layer_ids, layer_kappa, slot_order):
    counts = tuple(lax.axis_size(axis) for axis in ("gx", "gy", "gz"))
    nx, ny, nz = counts
    vectors, ex, ey, ez = probe_vectors.shape
    layers = layer_kappa.shape[0]
    groups = vectors // 8
    vmem = pl.BlockSpec(memory_space=pltpu.VMEM)
    smem = pl.BlockSpec(memory_space=pltpu.SMEM)
    phases = PASSES + 1
    longest = max(counts)
    blocks = pl.pallas_call(
        functools.partial(basis_kernel, counts, (ex, ey, ez), vectors, layers),
        out_shape=jax.ShapeDtypeStruct((nz, nx, ny, vectors, LANES), jnp.float32),
        in_specs=[vmem, vmem, smem],
        out_specs=vmem,
        scratch_shapes=[
            pltpu.VMEM((phases, ex + 2, ey + 2, groups + 1, 8, ez), jnp.float32),
            pltpu.VMEM((phases, 2, groups + 1, 8, ez), jnp.float32),
            pltpu.VMEM((phases, 2, groups + 1, 8, ez), jnp.float32),
            pltpu.VMEM((7, ex * ey, 8, ez), jnp.float32),
            pltpu.SemaphoreType.DMA((phases, 6)),
            pltpu.SemaphoreType.DMA((phases, 6)),
            pltpu.SemaphoreType.DMA((3, longest)),
            pltpu.SemaphoreType.DMA((3, longest)),
            pltpu.SemaphoreType.DMA((longest,)),
            pltpu.SemaphoreType.DMA((longest,)),
        ],
        compiler_params=pltpu.CompilerParams(
            collective_id=0, has_side_effects=True, vmem_limit_bytes=48 * 1024 * 1024
        ),
        name="basis",
    )(probe_vectors.reshape(vectors * ex * ey, ez), layer_ids.reshape(ex * ey, ez), layer_kappa)

    rows_local, cols_local = nz * vectors, nx * ny * vectors
    width = NPAN * min(PANEL, rows_local, cols_local)
    return pl.pallas_call(
        functools.partial(factor_kernel, counts, vectors, width, rows_local, cols_local),
        out_shape=jax.ShapeDtypeStruct((rows_local, cols_local), jnp.float32),
        in_specs=[smem, vmem],
        out_specs=vmem,
        scratch_shapes=[
            pltpu.SMEM((nx * ny * nz,), jnp.int32),
            pltpu.VMEM((width, width + cols_local + rows_local), jnp.float32),
            pltpu.VMEM((rows_local, cols_local), jnp.float32),
            pltpu.VMEM((width, LANES), jnp.float32),
        ],
        compiler_params=pltpu.CompilerParams(vmem_limit_bytes=48 * 1024 * 1024),
        name="factor",
    )(slot_order.reshape(-1), blocks)


def solution(mesh):
    in_specs = (P(None, "gx", "gy", "gz"), P("gx", "gy", "gz"), P(), P())
    out_specs = P(("gx", "gy"), "gz")
    return jax.shard_map(
        on_device, mesh=mesh, in_specs=in_specs, out_specs=out_specs, check_vma=False
    )
```

time: 455 us -> 59.6 us (0.13)
  waiting for transfers between devices: 220 us -> 0 us
  starting transfers between devices: 98.7 us -> 0 us
  other arithmetic: 61.5 us -> 0 us
  Pallas kernels: 0 us -> 56.6 us
  blocking collectives: 41.3 us -> 0 us
  between operations: 14.1 us -> 0.01 us
  local copies, waits for them, and re-layouts: 12.6 us -> 2.36 us
  matrix products: 5.55 us -> 0 us
    psum x4 -> x0, waiting for transfers between devices: 191 us -> none  [from_root(): return lax.psum(kept, axis)]
    ppermute x36 -> x0, starting transfers between devices: 98.4 us -> none  [the longest x18 75.1 us: with_halo(): lax.ppermute(lax.slice_in_dim(block, block.shape[dim] - width, None, axis...]
    pallas_call x0 -> x2, Pallas kernels: none -> 56.6 us  [the longest x1 35.1 us: on_device(): pl.pallas_call(functools.partial(basis_kernel, counts, (ex, ey, ez), vect...]
    another operation x11 -> x0, other arithmetic: 46.4 us -> none  [the longest x6 24.8 us: on_device(): factor = jnp.linalg.cholesky(diagonal_piece)]
    all_gather x2 -> x0, blocking collectives: 41.3 us -> none  [the longest x1 29.9 us: on_device(): piece = lax.all_gather(blocks[None], ('gx', 'gy'), axis=0, tiled=True)]
    ppermute x36 -> x0, waiting for transfers between devices: 28.5 us -> none  [the longest x18 15.5 us: with_halo(): lax.ppermute(lax.slice_in_dim(block, 0, width, axis=dim), axis, backward)]
    slice x31 -> x0, local copies, waits for them, and re-layouts: 5.01 us -> none  [the longest x11 2.75 us: with_halo(): lax.slice_in_dim(block, 0, width, axis=dim)]
    select_n x6 -> x0, other arithmetic: 4.75 us -> none  [from_root(): jnp.where(lax.axis_index(axis) == source, value, 0).astype(value.dtype)]
  transfers between devices with their start and end apart: 40 -> 0, of which waited for: 23 -> 0; matrix products, arithmetic and copies ran while one was open for 3% -> 0% of each run, Pallas kernels for 0% -> 0%
where the time goes in v1:
time: 59.6 us; the launch traced here: 59 us
  Pallas kernels  56.6 us (95%)
  local copies, waits for them, and re-layouts  2.36 us (4%)
    pallas_call x1, Pallas kernels, on_device(): pl.pallas_call(functools.partial(basis_kernel, counts, (ex, ey, ez), vect...  35.1 us
    pallas_call x1, Pallas kernels, on_device(): pl.pallas_call(functools.partial(factor_kernel, counts, vectors, width, r...  21.6 us
    unnamed x9, local copies, waits for them, and re-layouts  2.28 us

profile of v1, /device:TPU:0, one launch (start us, length us, event | category | flops | bytes accessed | tf_op | source)
XLA Modules:
  0.0 59.0 jit_solution(24801254985181596)
XLA Ops:
  0.0 0.0 copy-start.3
  0.0 0.0 copy-start.1
  0.0 0.7 %copy-done.3 = s32[8,4]{0,1:T(4,128)S(1)} copy-done((s32[8,4]{0,1:T(4,128)S(1)}, s32[8,4]{0,1:T(4,128)}, u32[]{:S(2)}) %copy-start.3) | copy-done | bytes 152
  0.7 0.1 copy.6
  0.8 0.0 copy-start.2
  0.8 0.1 reshape.9.slot_ref
  0.8 0.0 copy-done.1
  0.8 0.6 copy-done.2
  1.4 0.0 copy-start
  1.4 0.9 %copy-done = f32[32,2,8,128]{3,2,1,0:T(8,128)S(1)} copy-done((f32[32,2,8,128]{3,2,1,0:T(8,128)S(1)}, f32[32,2,8,128]{3,2,1,0:T(8,128)}, u32[]{:S(2)}) %copy-start) | copy-done | bytes 262168
  2.4 35.1 %basis.1.blocks_ref = f32[4,2,4,32,128]{4,3,2,1,0:T(8,128)S(1)} custom-call(f32[512,128]{1,0:T(8,128)S(1)} %bitcast.2, s32[16,128]{1,0:T(8,128)S(1)} %bitcast.3, f32[16]{0:T(128)S(1)} %copy-done.2), custom_call_target="tpu_custom_call" | custom-call | tf_op jit(solution)/shard_map/basis/pallas_call | solution.py:422
  37.5 21.6 %factor.1 = f32[128,256]{1,0:T(8,128)} custom-call(s32[32]{0:T(128)S(1)} %reshape.9.slot_ref, f32[4,2,4,32,128]{4,3,2,1,0:T(8,128)S(1)} %basis.1.blocks_ref), custom_call_target="tpu_custom_call" | custom-call | tf_op jit(solution)/shard_map/factor/pallas_call | solution.py:447
Async XLA Ops:
  0.0 0.7 %copy-start.3 = (s32[8,4]{0,1:T(4,128)S(1)}, s32[8,4]{0,1:T(4,128)}, u32[]{:S(2)}) copy-start(s32[8,4]{0,1:T(4,128)} %param.7) | copy-start | bytes 388
  0.0 0.8 %copy-start.1 = (s32[2,8,128]{2,1,0:T(8,128)S(1)}, s32[2,8,128]{2,1,0:T(8,128)}, u32[]{:S(2)}) copy-start(s32[2,8,128]{2,1,0:T(8,128)} %param.5) | copy-start | bytes 24580
  0.8 0.7 %copy-start.2 = (f32[16]{0:T(128)S(1)}, f32[16]{0:T(128)}, u32[]{:S(2)}) copy-start(f32[16]{0:T(128)} %kappa_ref.1) | copy-start | bytes 196
  1.4 0.9 %copy-start = (f32[32,2,8,128]{3,2,1,0:T(8,128)S(1)}, f32[32,2,8,128]{3,2,1,0:T(8,128)}, u32[]{:S(2)}) copy-start(f32[32,2,8,128]{3,2,1,0:T(8,128)} %param.4) | copy-start | bytes 786436

commit v2 on v1

--- a/solution.py
+++ b/solution.py
@@ -269,129 +269,155 @@
                 copy_of(phase, side).wait_send()
 
 
+def split(value):
+    high = value.astype(jnp.bfloat16)
+    rest = value - high.astype(jnp.float32)
+    middle = rest.astype(jnp.bfloat16)
+    return high, middle, (rest - middle.astype(jnp.float32)).astype(jnp.bfloat16)
+
+
+def left_stack(value):
+    high, middle, low = split(value)
+    return jnp.concatenate([high, high, middle, high, low, middle], axis=0)
+
+
+def right_stack(value):
+    high, middle, low = split(value)
+    return jnp.concatenate([high, middle, high, low, high, middle], axis=0)
+
+
 def factor_kernel(
     counts, vectors, width, rows_local, cols_local,
-    slot_ref, blocks_ref, out_ref, place, panel, local, pivots,
+    slot_ref, blocks_ref, out_ref, place, strips, panel, local, across,
 ):
     nx, ny, nz = counts
     ix, iy, iz = lax.axis_index("gx"), lax.axis_index("gy"), lax.axis_index("gz")
     rows_total = nx * ny
+    devices = rows_total * nz
     row_block = (ix * ny + iy) * (rows_local // vectors)
-    col_block = iz * (cols_local // vectors)
     wide = width // vectors
     per_tile = LANES // vectors
+    own_cols = pl.ds(pl.multiple_of(iz * cols_local, LANES), cols_local)
+    own_rows = pl.ds(pl.multiple_of(row_block * vectors, LANES), rows_local)
 
     def note(s, carry):
         place[slot_ref[s]] = s
         return carry
 
-    lax.fori_loop(0, rows_total * nz, note, 0)
-    panel[...] = jnp.zeros(panel.shape, jnp.float32)
-    local[...] = jnp.zeros(local.shape, jnp.float32)
+    lax.fori_loop(0, devices, note, 0, unroll=8)
     lane = lax.broadcasted_iota(jnp.int32, (vectors, LANES), 1)
-
-    def put(ref, row_at, col_at, value):
-        rows = pl.ds(pl.multiple_of(row_at * vectors, vectors), vectors)
-        cols = pl.ds(pl.multiple_of((col_at // per_tile) * LANES, LANES), LANES)
-        ref[rows, cols] += pltpu.roll(value, (col_at % per_tile) * vectors, 1)
-
-    def block_row(q, store):
+    filler = jnp.zeros((LANES - 3 * vectors, LANES), jnp.float32)
+
+    def block_row(q, at):
+        strip = strips.at[at]
+        strip[...] = jnp.zeros(strip.shape, jnp.float32)
         s = place[q]
         r, l = s // nz, s % nz
         i, j = r // ny, r % ny
-        steps = ((ny, 0, i < nx - 1, i > 0), (1, 0, j < ny - 1, j > 0), (0, 1, l < nz - 1, l > 0))
+
+        def put(c, value, lane_at):
+            cols = pl.ds(pl.multiple_of((c // per_tile) * LANES, LANES), LANES)
+            begin = (c % per_tile) * vectors
+            moved = pltpu.roll(value, lax.rem(begin + LANES - lane_at, LANES), 1)
+            pltpu.store(
+                strip.at[:, cols], moved, mask=(lane >= begin) & (lane < begin + vectors)
+            )
+
         mine = blocks_ref[l, i, j]
-        store(q, jnp.where(lane < vectors, mine, 0.0))
-        for face, (dr, dl, up, down) in enumerate(steps):
-            @pl.when(up)
-            def _():
-                value = pltpu.roll(mine, LANES - (face + 1) * vectors, 1)
-                store(slot_ref[(r + dr) * nz + l + dl], jnp.where(lane < vectors, value, 0.0))
-
-            @pl.when(down)
-            def _():
-                r2, l2 = r - dr, l - dl
-                other = blocks_ref[l2, r2 // ny, r2 % ny]
-                square = jnp.concatenate(
-                    [other, jnp.zeros((LANES - vectors, LANES), jnp.float32)], axis=0
-                )
-                at = (face + 1) * vectors
-                store(slot_ref[r2 * nz + l2], square.T[at : at + vectors, :])
+        put(q, mine, 0)
+        faces = ((ny, 0, i < nx - 1, i > 0), (1, 0, j < ny - 1, j > 0), (0, 1, l < nz - 1, l > 0))
+        below = []
+        lower = []
+        for face, (dr, dl, up, down) in enumerate(faces):
+            n = jnp.where(up, s + dr * nz + dl, s)
+            put(jnp.where(up, slot_ref[n], devices), mine, (face + 1) * vectors)
+            n = jnp.where(down, s - dr * nz - dl, s)
+            lower.append(jnp.where(down, slot_ref[n], devices))
+            r2, l2 = n // nz, n % nz
+            below.append(pltpu.roll(blocks_ref[l2, r2 // ny, r2 % ny], LANES - (face + 1) * vectors, 1))
+        turned = jnp.concatenate(below + [filler], axis=0).T[:vectors, :]
+        for face in range(3):
+            put(lower[face], turned, face * vectors)
+        return strip
 
     def top_row(q, carry):
-        def store(c, value):
-            pl.when(c < wide)(lambda: put(panel, q, c, value))
-            pl.when((c >= col_block) & (c < col_block + cols_local // vectors))(
-                lambda: put(panel, q, wide + c - col_block, value)
-            )
-            pl.when((c >= row_block) & (c < row_block + rows_local // vectors))(
-                lambda: put(panel, q, wide + cols_local // vectors + c - row_block, value)
-            )
-
-        block_row(q, store)
+        strip = block_row(q, q % 4)
+        rows = pl.ds(pl.multiple_of(q * vectors, vectors), vectors)
+        panel[rows, :width] = strip[:, :width]
+        panel[rows, width : width + cols_local] = strip[:, own_cols]
+        panel[rows, width + cols_local :] = strip[:, own_rows]
         return carry
 
     def own_row(n, carry):
-        def store(c, value):
-            pl.when((c >= col_block) & (c < col_block + cols_local // vectors))(
-                lambda: put(local, n, c - col_block, value)
-            )
-
-        block_row(row_block + n, store)
+        strip = block_row(row_block + n, n % 4)
+        rows = pl.ds(pl.multiple_of(n * vectors, vectors), vectors)
+        local[rows, :] = strip[:, own_cols]
         return carry
 
-    lax.fori_loop(0, wide, top_row, 0)
-    lax.fori_loop(0, rows_local // vectors, own_row, 0)
-
-    row8 = lax.broadcasted_iota(jnp.int32, (vectors, LANES), 0)
-
-    def eliminate(b, carry):
-        rows = pl.ds(pl.multiple_of(b * vectors, vectors), vectors)
-        tile = pl.ds(pl.multiple_of((b // per_tile) * LANES, LANES), LANES)
-        near = pltpu.roll(panel[rows, tile], (LANES - (b % per_tile) * vectors) % LANES, 1)
-        body = panel[rows, :]
-        pivot = jnp.ones((vectors, LANES), jnp.float32)
-        inverse = jnp.ones((vectors, LANES), jnp.float32)
-        for first in range(0, vectors, 8):
+    lax.fori_loop(0, wide, top_row, 0, unroll=4)
+    lax.fori_loop(0, rows_local // vectors, own_row, 0, unroll=4)
+
+    row = lax.broadcasted_iota(jnp.int32, (8, LANES), 0)
+    groups = vectors // 8
+
+    def times(left, right):
+        return lax.dot_general(
+            left, right, (((0,), (0,)), ((), ())), preferred_element_type=jnp.float32
+        )
+
+    for b in range(wide):
+        begin = (b // per_tile) * LANES
+        lane_at = (b % per_tile) * vectors
+        body = [panel[b * vectors + 8 * g : b * vectors + 8 * g + 8, begin:] for g in range(groups)]
+        tiles = body[0].shape[1] // LANES
+        pivots, inverses = [], []
+        for g in range(groups):
+            pivot = jnp.ones((8, LANES), jnp.float32)
+            inverse = pivot
             columns = [
-                jnp.broadcast_to(near[:, first + t : first + t + 1], (vectors, LANES)) for t in range(8)
+                [
+                    jnp.broadcast_to(
+                        body[h][:, lane_at + 8 * g + t : lane_at + 8 * g + t + 1], (8, LANES)
+                    )
+                    for h in range(g, groups)
+                ]
+                for t in range(8)
             ]
             for t in range(8):
-                j = first + t
-                head = columns[t][j : j + 1, :]
+                head = columns[t][0][t : t + 1, :]
                 turn = 1.0 / head
-                pivot = jnp.where(row8 == j, head, pivot)
-                inverse = jnp.where(row8 == j, turn, inverse)
-                factor = jnp.where(row8 > j, columns[t] * turn, 0.0)
+                pivot = jnp.where(row == t, head, pivot)
+                inverse = jnp.where(row == t, turn, inverse)
+                kept = [jnp.where(row > t, columns[t][0], 0.0)] + columns[t][1:]
                 for u in range(t + 1, 8):
-                    columns[u] = columns[u] - factor * columns[u][j : j + 1, :]
-                near = near - factor * near[j : j + 1, :]
-                spread = jnp.concatenate([factor] * (body.shape[1] // LANES), axis=1)
-                body = body - spread * body[j : j + 1, :]
-        panel[rows, :] = body
-        pivots[rows, :] = pivot
-
-        scaled = jnp.concatenate([inverse] * (width // LANES), axis=1) * body[:, :width]
-        column = lax.broadcasted_iota(jnp.int32, scaled.shape, 1)
-        scaled = jnp.where(column >= (b + 1) * vectors, scaled, 0.0)
-        panel[...] -= jnp.dot(
-            scaled.T, body, precision=HIGHEST, preferred_element_type=jnp.float32
+                    across_row = columns[u][0][t : t + 1, :]
+                    columns[u] = [
+                        value - (part * across_row) * turn for value, part in zip(columns[u], kept)
+                    ]
+                body_row = body[g][t : t + 1, :]
+                for h in range(g, groups):
+                    factor = kept[h - g] * turn
+                    body[h] = body[h] - jnp.concatenate([factor] * tiles, axis=1) * body_row
+            pivots.append(pivot)
+            inverses.append(inverse)
+        strip = jnp.concatenate(body, axis=0)
+        pivot = jnp.concatenate(pivots, axis=0)
+        inverse = jnp.concatenate(inverses, axis=0)
+        mine = strip[:, width + cols_local - begin :]
+        across[b * vectors : (b + 1) * vectors, :] = mine * jnp.concatenate(
+            [lax.rsqrt(pivot)] * (rows_local // LANES), axis=1
         )
-        return carry
-
-    lax.fori_loop(0, wide, eliminate, 0)
-
-    scale = lax.rsqrt(pivots[...])
-    for tile in range(panel.shape[1] // LANES):
-        if tile >= width // LANES:
-            at = slice(tile * LANES, (tile + 1) * LANES)
-            panel[:, at] = panel[:, at] * scale
-
-    across = panel[:, width + cols_local :].T
-    update = jnp.dot(
-        across, panel[:, width : width + cols_local],
-        precision=HIGHEST, preferred_element_type=jnp.float32,
-    )
+        right = right_stack(strip)
+        left_of = lambda value: left_stack(
+            value * jnp.concatenate([inverse] * (value.shape[1] // LANES), axis=1)
+        )
+        for tile in range((b + 1) // per_tile, width // LANES):
+            at = tile * LANES
+            change = times(left_of(strip[:, at - begin : at - begin + LANES]), right[:, at - begin :])
+            first = max((b + 1) * vectors, at)
+            panel[first : at + LANES, at:] -= change[first - at :, :]
+        local[...] -= times(left_of(mine), right[:, width - begin : width + cols_local - begin])
+
     row_ids = row_block * vectors + lax.broadcasted_iota(jnp.int32, (rows_local, LANES), 0)
     for tile in range(cols_local // LANES):
         at = slice(tile * LANES, (tile + 1) * LANES)
@@ -400,13 +426,12 @@
 
         @pl.when(start < width)
         def _():
-            part = panel[pl.ds(pl.multiple_of(start, LANES), LANES), width + cols_local :]
+            part = across[pl.ds(pl.multiple_of(start, LANES), LANES), :]
             out_ref[:, at] = jnp.where(col_ids <= row_ids, part.T, 0.0)
 
         @pl.when(start >= width)
         def _():
-            rest = local[:, at] - update[:, at]
-            out_ref[:, at] = jnp.where(row_ids >= width, rest, 0.0)
+            out_ref[:, at] = jnp.where(row_ids >= width, local[:, at], 0.0)
 
 
 def on_device(probe_vectors, layer_ids, layer_kappa, slot_order):
@@ -451,9 +476,10 @@
         out_specs=vmem,
         scratch_shapes=[
             pltpu.SMEM((nx * ny * nz,), jnp.int32),
+            pltpu.VMEM((4, vectors, nx * ny * nz * vectors + LANES), jnp.float32),
             pltpu.VMEM((width, width + cols_local + rows_local), jnp.float32),
             pltpu.VMEM((rows_local, cols_local), jnp.float32),
-            pltpu.VMEM((width, LANES), jnp.float32),
+            pltpu.VMEM((width, rows_local), jnp.float32),
         ],
         compiler_params=pltpu.CompilerParams(vmem_limit_bytes=48 * 1024 * 1024),
         name="factor",

time: 59.6 us -> 48.4 us (0.81)
  Pallas kernels: 56.6 us -> 45.8 us
    pallas_call x1, Pallas kernels: 21.6 us -> 10.7 us  [on_device(): pl.pallas_call(functools.partial(factor_kernel, counts, vectors, width, r...]
where the time goes in v2:
time: 48.4 us; the launch traced here: 48.2 us
  Pallas kernels  45.8 us (95%)
  local copies, waits for them, and re-layouts  2.36 us (5%)
    pallas_call x1, Pallas kernels, on_device(): pl.pallas_call(functools.partial(basis_kernel, counts, (ex, ey, ez), vect...  35.1 us
    pallas_call x1, Pallas kernels, on_device(): pl.pallas_call(functools.partial(factor_kernel, counts, vectors, width, r...  10.7 us
    unnamed x9, local copies, waits for them, and re-layouts  2.28 us

profile of v2, /device:TPU:0, one launch (start us, length us, event | category | flops | bytes accessed | tf_op | source)
XLA Modules:
  0.0 48.2 jit_solution(10721293292804404017)
XLA Ops:
  0.0 0.0 copy-start.3
  0.0 0.0 copy-start.1
  0.0 0.7 %copy-done.3 = s32[8,4]{0,1:T(4,128)S(1)} copy-done((s32[8,4]{0,1:T(4,128)S(1)}, s32[8,4]{0,1:T(4,128)}, u32[]{:S(2)}) %copy-start.3) | copy-done | bytes 152
  0.7 0.1 copy.6
  0.8 0.0 copy-start.2
  0.8 0.1 reshape.9.slot_ref
  0.8 0.0 copy-done.1
  0.8 0.6 %copy-done.2 = f32[16]{0:T(128)S(1)} copy-done((f32[16]{0:T(128)S(1)}, f32[16]{0:T(128)}, u32[]{:S(2)}) %copy-start.2) | copy-done | bytes 88
  1.4 0.0 copy-start
  1.4 0.9 %copy-done = f32[32,2,8,128]{3,2,1,0:T(8,128)S(1)} copy-done((f32[32,2,8,128]{3,2,1,0:T(8,128)S(1)}, f32[32,2,8,128]{3,2,1,0:T(8,128)}, u32[]{:S(2)}) %copy-start) | copy-done | bytes 262168
  2.4 35.1 %basis.1.blocks_ref = f32[4,2,4,32,128]{4,3,2,1,0:T(8,128)S(1)} custom-call(f32[512,128]{1,0:T(8,128)S(1)} %bitcast.2, s32[16,128]{1,0:T(8,128)S(1)} %bitcast.3, f32[16]{0:T(128)S(1)} %copy-done.2), custom_call_target="tpu_custom_call" | custom-call | tf_op jit(solution)/shard_map/basis/pallas_call | solution.py:447
  37.5 10.7 %factor.1 = f32[128,256]{1,0:T(8,128)} custom-call(s32[32]{0:T(128)S(1)} %reshape.9.slot_ref, f32[4,2,4,32,128]{4,3,2,1,0:T(8,128)S(1)} %basis.1.blocks_ref), custom_call_target="tpu_custom_call" | custom-call | tf_op jit(solution)/shard_map/factor/pallas_call | solution.py:472
Async XLA Ops:
  0.0 0.7 %copy-start.3 = (s32[8,4]{0,1:T(4,128)S(1)}, s32[8,4]{0,1:T(4,128)}, u32[]{:S(2)}) copy-start(s32[8,4]{0,1:T(4,128)} %param.7) | copy-start | bytes 388
  0.0 0.8 %copy-start.1 = (s32[2,8,128]{2,1,0:T(8,128)S(1)}, s32[2,8,128]{2,1,0:T(8,128)}, u32[]{:S(2)}) copy-start(s32[2,8,128]{2,1,0:T(8,128)} %param.5) | copy-start | bytes 24580
  0.8 0.7 %copy-start.2 = (f32[16]{0:T(128)S(1)}, f32[16]{0:T(128)}, u32[]{:S(2)}) copy-start(f32[16]{0:T(128)} %kappa_ref.1) | copy-start | bytes 196
  1.4 0.9 %copy-start = (f32[32,2,8,128]{3,2,1,0:T(8,128)S(1)}, f32[32,2,8,128]{3,2,1,0:T(8,128)}, u32[]{:S(2)}) copy-start(f32[32,2,8,128]{3,2,1,0:T(8,128)} %param.4) | copy-start | bytes 786436

commit v3 on v2

--- a/solution.py
+++ b/solution.py
@@ -37,9 +37,9 @@
 
 def basis_kernel(
     counts, extents, vectors, layers,
-    probe_ref, ids_ref, kappa_ref, out_ref,
-    field, zsend, zrecv, weight, send_sem, recv_sem,
-    line_send, line_recv, own_send, own_recv,
+    probe_hbm, ids_hbm, kappa_hbm, out_ref,
+    probe, ids, kappa_ref, field, zsend, zrecv, zghost, weight, weight_z,
+    load_sem, send_sem, recv_sem, y_send, y_recv, z_send, z_recv, x_send, x_recv,
 ):
     nx, ny, nz = counts
     ex, ey, ez = extents
@@ -48,6 +48,13 @@
     ix, iy, iz = lax.axis_index("gx"), lax.axis_index("gy"), lax.axis_index("gz")
     lines = (("gx", ix, nx), ("gy", iy, ny), ("gz", iz, nz))
 
+    loads = [
+        pltpu.make_async_copy(src, dst, load_sem.at[n])
+        for n, (src, dst) in enumerate(((probe_hbm, probe), (ids_hbm, ids), (kappa_hbm, kappa_ref)))
+    ]
+    for load in loads:
+        load.start()
+
     barrier = pltpu.get_barrier_semaphore()
     for axis, index, count in lines:
         for step in range(1, count):
@@ -56,20 +63,8 @@
             )
 
     lane = lax.broadcasted_iota(jnp.int32, (1, 8, ez), 2)
+    even = lane % 2 == 0
     zero_plane = jnp.zeros((groups + 1, 8, ez), jnp.float32)
-
-    ids = ids_ref[...]
-    kappa = jnp.zeros(ids.shape, jnp.float32)
-    for layer in range(layers):
-        kappa = jnp.where(ids == layer, kappa_ref[layer], kappa)
-    for x in range(ex):
-        for y in range(ey):
-            k = x * ey + y
-            field[0, x + 1, y + 1, 0:groups] = probe_ref[
-                pl.ds(k, vectors, stride=cells), :
-            ].reshape(groups, 8, ez)
-            field[0, x + 1, y + 1, groups] = jnp.broadcast_to(kappa[k : k + 1, :], (8, ez))
-
     inside = (ix > 0, ix < nx - 1, iy > 0, iy < ny - 1, iz > 0, iz < nz - 1)
 
     def clear(side, phase):
@@ -87,6 +82,13 @@
         def _():
             for phase in range(PASSES + 1):
                 clear(side, phase)
+
+    def number(x, y):
+        return (x - 1) * ey + y - 1
+
+    every = [(x, y) for y in range(1, ey + 1) for x in range(1, ex + 1)]
+    order = [at for at in every if at[1] in (1, ey)] + [at for at in every if at[1] not in (1, ey)]
+    edges = len([at for at in every if at[1] in (1, ey)])
 
     def copy_of(phase, side):
         span = pl.ds(0, groups + 1 if phase == 0 else groups)
@@ -100,7 +102,7 @@
             src = field.at[phase, pl.ds(1, ex), 1 if low else ey, span]
             dst = field.at[phase, pl.ds(1, ex), ey + 1 if low else 0, span]
         else:
-            src = zsend.at[phase, 0 if low else 1, span]
+            src = zsend.at[phase, span]
             dst = zrecv.at[phase, 1 if low else 0, span]
         return pltpu.make_async_remote_copy(
             src_ref=src, dst_ref=dst,
@@ -108,165 +110,238 @@
             device_id={axis: target}, device_id_type=MESH,
         )
 
-    def sides_of(phase):
-        return range(6) if phase < PASSES else (0, 2, 4)
-
-    def send(phase):
-        span = groups + 1 if phase == 0 else groups
-        for low in ((True, False) if phase < PASSES else (True,)):
-            packed = jnp.zeros((span, 8, ez), jnp.float32)
-            for x in range(ex):
-                for y in range(ey):
-                    k = x * ey + y
-                    value = field[phase, x + 1, y + 1, 0:span]
-                    shift = k if low else k + 1
-                    if shift:
-                        value = pltpu.roll(value, shift, 2)
-                    packed = jnp.where(lane == k, value, packed)
-            zsend[phase, 0 if low else 1, 0:span] = packed
-        for side in sides_of(phase):
+    def sides_of(phase, axis):
+        return (2 * axis, 2 * axis + 1) if phase < PASSES else (2 * axis,)
+
+    def send(phase, axis):
+        for side in sides_of(phase, axis):
             @pl.when(inside[side])
             def _():
                 copy_of(phase, side).start()
 
-    def receive(phase):
-        for side in sides_of(phase):
+    def receive(phase, axis):
+        for side in sides_of(phase, axis):
             @pl.when(inside[side ^ 1])
             def _():
                 copy_of(phase, side).wait_recv()
 
-    def z_neighbours(phase, k, value, part):
-        span = value.shape[0]
-        above = pltpu.roll(value, ez - 1, 2)
-        ghost = zrecv[phase, 1, part : part + span]
-        if (ez - 1 - k) % ez:
-            ghost = pltpu.roll(ghost, ez - 1 - k, 2)
-        above = jnp.where(lane == ez - 1, ghost, above)
+    def packed(values, span):
+        total = jnp.zeros((span, 8, ez), jnp.float32)
+        for (x, y), value in values:
+            k = number(x, y)
+            turned = pltpu.roll(value, 2 * k, 2) if k else value
+            total = jnp.where((lane == 2 * k) | (lane == (2 * k - 1) % ez), turned, total)
+        return total
+
+    def unpack(phase, span):
+        above = pltpu.roll(zrecv[phase, 1, 0:span], ez - 1, 2)
         if phase == PASSES:
-            return above, None
-        below = pltpu.roll(value, 1, 2)
-        ghost = zrecv[phase, 0, part : part + span]
-        if k:
-            ghost = pltpu.roll(ghost, ez - k, 2)
-        return above, jnp.where(lane == 0, ghost, below)
+            return jnp.where(even, 0.0, above)
+        return jnp.where(even, pltpu.roll(zrecv[phase, 0, 0:span], 1, 2), above)
+
+    def ghost_of(value, k):
+        return pltpu.roll(value, ez - 2 * k, 2) if k else value
+
+    slope = 2.0 / (UPPER_EDGE - LOWER_EDGE)
+    shift = (UPPER_EDGE + LOWER_EDGE) / (UPPER_EDGE - LOWER_EDGE)
+    steps = ((1, 0), (-1, 0), (0, 1), (0, -1))
+
+    def is_ghost(x, y, face):
+        x2, y2 = x + steps[face][0], y + steps[face][1]
+        return x2 in (0, ex + 1) or y2 in (0, ey + 1)
+
+    def beside(phase, x, y, face):
+        return field[phase, x + steps[face][0], y + steps[face][1], 0:groups]
+
+    for load in loads:
+        load.wait()
+    for x, y in every:
+        k = number(x, y)
+        field[0, x, y, 0:groups] = probe[pl.ds(k, vectors, stride=cells), :].reshape(groups, 8, ez)
+    for x in range(1, ex + 1):
+        layer_of = ids[x - 1]
+        kappa = jnp.zeros(layer_of.shape, jnp.float32)
+        for layer in range(layers):
+            kappa = jnp.where(layer_of == layer, kappa_ref[layer], kappa)
+        for y in range(1, ey + 1):
+            field[0, x, y, groups] = jnp.broadcast_to(kappa[y - 1 : y, :], (8, ez))
 
     pl.semaphore_wait(barrier, sum(count - 1 for _, _, count in lines))
+    send(0, 1)
+    zsend[0] = packed([((x, y), field[0, x, y]) for x, y in order], groups + 1)
+    send(0, 2)
+    send(0, 0)
+
+    half = 0.5 * slope
+
+    def kappa_at(x, y):
+        return field[0, x, y, groups]
+
+    def face_weight(x, y, face):
+        weight[face, number(x, y)] = half * (
+            kappa_at(x, y) + kappa_at(x + steps[face][0], y + steps[face][1])
+        )
+
+    flat = lane[0]
+    for x, y in order:
+        k = number(x, y)
+        for face in range(4):
+            if not is_ghost(x, y, face):
+                face_weight(x, y, face)
+        here = kappa_at(x, y)
+        weight[4, k] = jnp.where(flat == ez - 1, 0.0, half * (here + pltpu.roll(here, ez - 1, 1)))
+        weight[5, k] = jnp.where(flat == 0, 0.0, half * (here + pltpu.roll(here, 1, 1)))
 
     for phase in range(PASSES):
-        send(phase)
-        receive(phase)
+        factor_one, factor_two = cheb_factors(phase)
+        for x, y in order:
+            k = number(x, y)
+            here = field[phase, x, y, 0:groups]
+            value = shift * here
+            for face in range(4):
+                if not is_ghost(x, y, face):
+                    value += weight[face, k][None] * (beside(phase, x, y, face) - here)
+            value += weight[4, k][None] * (pltpu.roll(here, ez - 1, 2) - here)
+            value += weight[5, k][None] * (pltpu.roll(here, 1, 2) - here)
+            value = factor_one * value
+            if phase > 0:
+                value -= factor_two * field[phase - 1, x, y, 0:groups]
+            field[phase + 1, x, y, 0:groups] = value
+        for axis in range(3):
+            receive(phase, axis)
         if phase == 0:
-            for x in range(1, ex + 1):
-                for y in range(1, ey + 1):
-                    k = (x - 1) * ey + y - 1
-                    here = field[0, x, y, groups : groups + 1]
-                    above, below = z_neighbours(0, k, here, groups)
-                    beside = (
-                        field[0, x + 1, y, groups : groups + 1], field[0, x - 1, y, groups : groups + 1],
-                        field[0, x, y + 1, groups : groups + 1], field[0, x, y - 1, groups : groups + 1],
-                        above, below,
-                    )
-                    total = None
-                    for face in range(6):
-                        value = 0.5 * (here + beside[face])
-                        total = value if total is None else total + value
-                        weight[face, k] = value[0]
-                    weight[6, k] = total[0]
-        factor_one, factor_two = cheb_factors(phase)
-        shift = (UPPER_EDGE + LOWER_EDGE) / (UPPER_EDGE - LOWER_EDGE)
-        slope = 2.0 / (UPPER_EDGE - LOWER_EDGE)
-        for x in range(1, ex + 1):
-            for y in range(1, ey + 1):
-                k = (x - 1) * ey + y - 1
-                here = field[phase, x, y, 0:groups]
-                above, below = z_neighbours(phase, k, here, 0)
-                beside = weight[0, k][None] * field[phase, x + 1, y, 0:groups]
-                beside += weight[1, k][None] * field[phase, x - 1, y, 0:groups]
-                beside += weight[2, k][None] * field[phase, x, y + 1, 0:groups]
-                beside += weight[3, k][None] * field[phase, x, y - 1, 0:groups]
-                beside += weight[4, k][None] * above + weight[5, k][None] * below
-                applied = weight[6, k][None] * here - beside
-                value = factor_one * (shift * here - slope * applied)
-                if phase > 0:
-                    value -= factor_two * field[phase - 1, x, y, 0:groups]
-                field[phase + 1, x, y, 0:groups] = value
-
-    send(PASSES)
-    left, own = [], []
-    for x in range(1, ex + 1):
-        for y in range(1, ey + 1):
-            k = (x - 1) * ey + y - 1
-            here = field[PASSES, x, y, 0:groups]
-            image = weight[6, k][None] * here
-            if x < ex:
-                image -= weight[0, k][None] * field[PASSES, x + 1, y, 0:groups]
-            if x > 1:
-                image -= weight[1, k][None] * field[PASSES, x - 1, y, 0:groups]
-            if y < ey:
-                image -= weight[2, k][None] * field[PASSES, x, y + 1, 0:groups]
-            if y > 1:
-                image -= weight[3, k][None] * field[PASSES, x, y - 1, 0:groups]
-            above = jnp.where(lane == ez - 1, 0.0, pltpu.roll(here, ez - 1, 2))
-            below = jnp.where(lane == 0, 0.0, pltpu.roll(here, 1, 2))
-            image -= weight[4, k][None] * above + weight[5, k][None] * below
-            left.append(here.reshape(vectors, ez))
-            own.append(image.reshape(vectors, ez))
-    receive(PASSES)
-    right = []
-    zeros = jnp.zeros((vectors, ez), jnp.float32)
-    for x in range(1, ex + 1):
-        for y in range(1, ey + 1):
-            k = (x - 1) * ey + y - 1
-            rows = [own[k], zeros, zeros]
-            if x == ex:
-                rows[1] = (-weight[0, k][None] * field[PASSES, x + 1, y, 0:groups]).reshape(vectors, ez)
-            if y == ey:
-                rows[2] = (-weight[2, k][None] * field[PASSES, x, y + 1, 0:groups]).reshape(vectors, ez)
-            ghost = zrecv[PASSES, 1, 0:groups]
-            if (ez - 1 - k) % ez:
-                ghost = pltpu.roll(ghost, ez - 1 - k, 2)
-            ghost = jnp.where(lane == ez - 1, -weight[4, k][None] * ghost, 0.0)
-            rows.append(ghost.reshape(vectors, ez))
-            right.append(jnp.concatenate(rows, axis=0))
-    product = lax.dot_general(
-        jnp.concatenate(left, axis=1), jnp.concatenate(right, axis=1),
-        (((1,), (1,)), ((), ())), precision=HIGHEST, preferred_element_type=jnp.float32,
-    ) * (1.0 / math.sqrt(cells * ez))
-    row = lax.broadcasted_iota(jnp.int32, product.shape, 0)
-    column = lax.broadcasted_iota(jnp.int32, product.shape, 1)
-    out_ref[iz, ix, iy] = product + jnp.where(row == column, COARSE_SHIFT, 0.0)
-
-    waits = []
-
-    def spread(axis, index, count, ref_of, sends, recvs):
-        copies = []
+            ghosts = unpack(0, groups + 1)
+            zsum = half * (zsend[0, groups] + ghosts[groups])
+            weight_z[...] = jnp.where(even[0], 0.0, zsum)
+            for x, y in order:
+                k = number(x, y)
+                for face in range(4):
+                    if is_ghost(x, y, face):
+                        face_weight(x, y, face)
+                value = half * (kappa_at(x, y) + ghost_of(ghosts[groups:], k)[0])
+                weight[6, k] = jnp.where((flat == 0) | (flat == ez - 1), value, 0.0)
+        zghost[...] = unpack(phase, groups)
+        done = []
+        for n, (x, y) in enumerate(order):
+            k = number(x, y)
+            here = field[phase, x, y, 0:groups]
+            value = weight[6, k][None] * (ghost_of(zghost[...], k) - here)
+            for face in range(4):
+                if is_ghost(x, y, face):
+                    value += weight[face, k][None] * (beside(phase, x, y, face) - here)
+            value = field[phase + 1, x, y, 0:groups] + factor_one * value
+            field[phase + 1, x, y, 0:groups] = value
+            if n == edges - 1:
+                send(phase + 1, 1)
+        zsend[phase + 1, 0:groups] = packed(
+            [((x, y), field[phase + 1, x, y, 0:groups]) for x, y in order], groups
+        )
+        send(phase + 1, 2)
+        send(phase + 1, 0)
+
+    def product(left, right):
+        return lax.dot_general(
+            jnp.concatenate([value.reshape(vectors, ez) for value in left], axis=1),
+            jnp.concatenate([value.reshape(vectors, ez) for value in right], axis=1),
+            (((1,), (1,)), ((), ())), precision=HIGHEST, preferred_element_type=jnp.float32,
+        )
+
+    last = lambda x, y: field[PASSES, x, y, 0:groups]
+    images = []
+    for x, y in every:
+        k = number(x, y)
+        here = last(x, y)
+        value = weight[6, k][None] * here
+        for face in range(4):
+            other = here if is_ghost(x, y, face) else here - beside(PASSES, x, y, face)
+            value += weight[face, k][None] * other
+        value += weight[4, k][None] * (here - pltpu.roll(here, ez - 1, 2))
+        value += weight[5, k][None] * (here - pltpu.roll(here, 1, 2))
+        images.append(value)
+    scale = 1.0 / (slope * math.sqrt(cells * ez))
+    own = scale * product([last(x, y) for x, y in every], images)
+    row = lax.broadcasted_iota(jnp.int32, own.shape, 0)
+    column = lax.broadcasted_iota(jnp.int32, own.shape, 1)
+    own += jnp.where(row == column, COARSE_SHIFT, 0.0)
+
+    for axis in range(3):
+        receive(PASSES, axis)
+    x_face = product(
+        [last(ex, y) for y in range(1, ey + 1)],
+        [weight[0, number(ex, y)][None] * beside(PASSES, ex, y, 0) for y in range(1, ey + 1)],
+    )
+    y_face = product(
+        [last(x, ey) for x in range(1, ex + 1)],
+        [weight[2, number(x, ey)][None] * beside(PASSES, x, ey, 2) for x in range(1, ex + 1)],
+    )
+    z_face = product([zsend[PASSES, 0:groups]], [weight_z[...][None] * unpack(PASSES, groups)])
+    out_ref[iz, ix, iy] = jnp.concatenate(
+        [own, -scale * x_face, -scale * y_face, -scale * z_face], axis=1
+    )
+
+    def spread(axis, index, count, source, sends, recvs, act):
         for step in range(1, count):
-            copy = pltpu.make_async_remote_copy(
-                src_ref=ref_of(index), dst_ref=ref_of(index),
-                send_sem=sends.at[step], recv_sem=recvs.at[step],
+            chunk = out_ref.at[source]
+            act(pltpu.make_async_remote_copy(
+                src_ref=chunk, dst_ref=chunk, send_sem=sends(step), recv_sem=recvs(step),
                 device_id={axis: lax.rem(index + step, count)}, device_id_type=MESH,
-            )
-            copy.start()
-            copies.append(copy)
-        for step in range(1, count):
-            source = ref_of(lax.rem(index + count - step, count))
-            pltpu.make_async_remote_copy(
-                src_ref=source, dst_ref=source,
-                send_sem=sends.at[step], recv_sem=recvs.at[step],
-                device_id={axis: lax.rem(index + step, count)}, device_id_type=MESH,
-            ).wait_recv()
-        waits.extend(copies)
-
-    spread("gy", iy, ny, lambda i: out_ref.at[iz, ix, i], line_send.at[0], line_recv.at[0])
-    spread("gz", iz, nz, lambda i: out_ref.at[i, ix], line_send.at[1], line_recv.at[1])
-    spread("gx", ix, nx, lambda i: out_ref.at[:, i], line_send.at[2], line_recv.at[2])
-    for copy in waits:
-        copy.wait_send()
+            ))
+
+    def back(index, step, count):
+        return lax.rem(index + count - step, count)
+
+    def along_x(dz, dy, act):
+        source = (back(iz, dz, nz), ix, back(iy, dy, ny))
+        spread("gx", ix, nx, source, lambda step: x_send.at[step, dz, dy],
+               lambda step: x_recv.at[step, dz, dy], act)
+
+    def along_z(dy, act):
+        source = (iz, ix, back(iy, dy, ny))
+        spread("gz", iz, nz, source, lambda step: z_send.at[step, dy],
+               lambda step: z_recv.at[step, dy], act)
+
+    def along_y(act):
+        spread("gy", iy, ny, (iz, ix, iy), lambda step: y_send.at[step],
+               lambda step: y_recv.at[step], act)
+
+    def arrived(source, send_at, recv_at, axis, index, count):
+        chunk = out_ref.at[source]
+        pltpu.make_async_remote_copy(
+            src_ref=chunk, dst_ref=chunk, send_sem=send_at, recv_sem=recv_at,
+            device_id={axis: lax.rem(index + 1, count)}, device_id_type=MESH,
+        ).wait_recv()
+
+    start = lambda copy: copy.start()
+    along_y(start)
+    along_z(0, start)
+    along_x(0, 0, start)
+    for dy in range(1, ny):
+        arrived((iz, ix, back(iy, dy, ny)), y_send.at[dy], y_recv.at[dy], "gy", iy, ny)
+        along_z(dy, start)
+        along_x(0, dy, start)
+    for dy in range(ny):
+        for dz in range(1, nz):
+            arrived((back(iz, dz, nz), ix, back(iy, dy, ny)), z_send.at[dz, dy], z_recv.at[dz, dy],
+                    "gz", iz, nz)
+            along_x(dz, dy, start)
+    for dy in range(ny):
+        for dz in range(nz):
+            for dx in range(1, nx):
+                arrived((back(iz, dz, nz), back(ix, dx, nx), back(iy, dy, ny)),
+                        x_send.at[dx, dz, dy], x_recv.at[dx, dz, dy], "gx", ix, nx)
+
+    finish = lambda copy: copy.wait_send()
+    along_y(finish)
+    for dy in range(ny):
+        along_z(dy, finish)
+        for dz in range(nz):
+            along_x(dz, dy, finish)
     for phase in range(PASSES + 1):
-        for side in sides_of(phase):
-            @pl.when(inside[side])
-            def _():
-                copy_of(phase, side).wait_send()
+        for axis in range(3):
+            for side in sides_of(phase, axis):
+                @pl.when(inside[side])
+                def _():
+                    copy_of(phase, side).wait_send()
 
 
 def split(value):
@@ -442,30 +517,32 @@
     groups = vectors // 8
     vmem = pl.BlockSpec(memory_space=pltpu.VMEM)
     smem = pl.BlockSpec(memory_space=pltpu.SMEM)
+    anywhere = pl.BlockSpec(memory_space=pl.ANY)
     phases = PASSES + 1
-    longest = max(counts)
+    dma = pltpu.SemaphoreType.DMA
     blocks = pl.pallas_call(
         functools.partial(basis_kernel, counts, (ex, ey, ez), vectors, layers),
         out_shape=jax.ShapeDtypeStruct((nz, nx, ny, vectors, LANES), jnp.float32),
-        in_specs=[vmem, vmem, smem],
+        in_specs=[anywhere] * 3,
         out_specs=vmem,
         scratch_shapes=[
+            pltpu.VMEM((vectors * ex * ey, ez), jnp.float32),
+            pltpu.VMEM((ex, ey, ez), jnp.int32),
+            pltpu.SMEM((layers,), jnp.float32),
             pltpu.VMEM((phases, ex + 2, ey + 2, groups + 1, 8, ez), jnp.float32),
+            pltpu.VMEM((phases, groups + 1, 8, ez), jnp.float32),
             pltpu.VMEM((phases, 2, groups + 1, 8, ez), jnp.float32),
-            pltpu.VMEM((phases, 2, groups + 1, 8, ez), jnp.float32),
+            pltpu.VMEM((groups, 8, ez), jnp.float32),
             pltpu.VMEM((7, ex * ey, 8, ez), jnp.float32),
-            pltpu.SemaphoreType.DMA((phases, 6)),
-            pltpu.SemaphoreType.DMA((phases, 6)),
-            pltpu.SemaphoreType.DMA((3, longest)),
-            pltpu.SemaphoreType.DMA((3, longest)),
-            pltpu.SemaphoreType.DMA((longest,)),
-            pltpu.SemaphoreType.DMA((longest,)),
+            pltpu.VMEM((8, ez), jnp.float32),
+            dma((3,)), dma((phases, 6)), dma((phases, 6)),
+            dma((ny,)), dma((ny,)), dma((nz, ny)), dma((nz, ny)), dma((nx, nz, ny)), dma((nx, nz, ny)),
         ],
         compiler_params=pltpu.CompilerParams(
             collective_id=0, has_side_effects=True, vmem_limit_bytes=48 * 1024 * 1024
         ),
         name="basis",
-    )(probe_vectors.reshape(vectors * ex * ey, ez), layer_ids.reshape(ex * ey, ez), layer_kappa)
+    )(probe_vectors.reshape(vectors * ex * ey, ez), layer_ids, layer_kappa)
 
     rows_local, cols_local = nz * vectors, nx * ny * vectors
     width = NPAN * min(PANEL, rows_local, cols_local)

time: 48.4 us -> 46.5 us (0.961)
  Pallas kernels: 45.8 us -> 43.9 us
    pallas_call x1, Pallas kernels: 35.1 us -> 33.2 us  [on_device(): pl.pallas_call(functools.partial(basis_kernel, counts, (ex, ey, ez), vect...]
    unnamed x9 -> x7, local copies, waits for them, and re-layouts: 2.28 us -> 2.29 us
where the time goes in v3:
time: 46.5 us; the launch traced here: 46.3 us
  Pallas kernels  43.9 us (94%)
  local copies, waits for them, and re-layouts  2.37 us (5%)
    pallas_call x1, Pallas kernels, on_device(): pl.pallas_call(functools.partial(basis_kernel, counts, (ex, ey, ez), vect...  33.2 us
    pallas_call x1, Pallas kernels, on_device(): pl.pallas_call(functools.partial(factor_kernel, counts, vectors, width, r...  10.7 us
    unnamed x7, local copies, waits for them, and re-layouts  2.29 us

profile of v3, /device:TPU:0, one launch (start us, length us, event | category | flops | bytes accessed | tf_op | source)
XLA Modules:
  0.0 46.3 jit_solution(9714134609214660074)
XLA Ops:
  0.0 0.0 copy-start.1
  0.0 0.8 %copy.6 = s32[8,4]{1,0:T(8,128)S(1)} copy(s32[8,4]{0,1:T(4,128)} %param.7) | data formatting | bytes 256 | tf_op args[3]
  0.8 0.0 copy-start.2
  0.8 0.1 reshape.6.slot_ref
  0.9 0.0 copy-done.1
  0.9 0.6 %copy-done.2 = f32[16]{0:T(128)S(1)} copy-done((f32[16]{0:T(128)S(1)}, f32[16]{0:T(128)}, u32[]{:S(2)}) %copy-start.2) | copy-done | bytes 88
  1.4 0.0 copy-start
  1.4 0.9 %copy-done = f32[32,2,8,128]{3,2,1,0:T(8,128)S(1)} copy-done((f32[32,2,8,128]{3,2,1,0:T(8,128)S(1)}, f32[32,2,8,128]{3,2,1,0:T(8,128)}, u32[]{:S(2)}) %copy-start) | copy-done | bytes 262168
  2.4 33.2 %basis.1.blocks_ref = f32[4,2,4,32,128]{4,3,2,1,0:T(8,128)S(1)} custom-call(f32[512,128]{1,0:T(8,128)S(1)} %bitcast.1, s32[2,8,128]{2,1,0:T(8,128)S(1)} %copy-done.1, f32[16]{0:T(128)S(1)} %copy-done.2), custom_call_target="tpu_custom_call" | custom-call | tf_op jit(solution)/shard_map/basis/pallas_call | solution.py:523
  35.6 10.7 %factor.1 = f32[128,256]{1,0:T(8,128)} custom-call(s32[32]{0:T(128)S(1)} %reshape.6.slot_ref, f32[4,2,4,32,128]{4,3,2,1,0:T(8,128)S(1)} %basis.1.blocks_ref), custom_call_target="tpu_custom_call" | custom-call | tf_op jit(solution)/shard_map/factor/pallas_call | solution.py:549
Async XLA Ops:
  0.0 0.9 %copy-start.1 = (s32[2,8,128]{2,1,0:T(8,128)S(1)}, s32[2,8,128]{2,1,0:T(8,128)}, u32[]{:S(2)}) copy-start(s32[2,8,128]{2,1,0:T(8,128)} %ids_hbm.1) | copy-start | bytes 24580
  0.8 0.7 %copy-start.2 = (f32[16]{0:T(128)S(1)}, f32[16]{0:T(128)}, u32[]{:S(2)}) copy-start(f32[16]{0:T(128)} %kappa_hbm.1) | copy-start | bytes 196
  1.4 0.9 %copy-start = (f32[32,2,8,128]{3,2,1,0:T(8,128)S(1)}, f32[32,2,8,128]{3,2,1,0:T(8,128)}, u32[]{:S(2)}) copy-start(f32[32,2,8,128]{3,2,1,0:T(8,128)} %param.4) | copy-start | bytes 786436

commit v4 on v3

--- a/solution.py
+++ b/solution.py
@@ -16,7 +16,6 @@
 COARSE_SHIFT = 1.0
 LANES = 128
 MESH = pl.DeviceIdType.MESH
-HIGHEST = lax.Precision.HIGHEST
 
 
 def cheb_factors(step_index):
@@ -233,51 +232,62 @@
             field[phase + 1, x, y, 0:groups] = value
             if n == edges - 1:
                 send(phase + 1, 1)
+        send(phase + 1, 0)
         zsend[phase + 1, 0:groups] = packed(
             [((x, y), field[phase + 1, x, y, 0:groups]) for x, y in order], groups
         )
         send(phase + 1, 2)
-        send(phase + 1, 0)
 
     def product(left, right):
+        left = jnp.concatenate(left, axis=1)
+        right = jnp.concatenate(right, axis=1)
+        left_high, right_high = left.astype(jnp.bfloat16), right.astype(jnp.bfloat16)
+        left_low = (left - left_high.astype(jnp.float32)).astype(jnp.bfloat16)
+        right_low = (right - right_high.astype(jnp.float32)).astype(jnp.bfloat16)
         return lax.dot_general(
-            jnp.concatenate([value.reshape(vectors, ez) for value in left], axis=1),
-            jnp.concatenate([value.reshape(vectors, ez) for value in right], axis=1),
-            (((1,), (1,)), ((), ())), precision=HIGHEST, preferred_element_type=jnp.float32,
-        )
-
-    last = lambda x, y: field[PASSES, x, y, 0:groups]
+            jnp.concatenate([left_high, left_high, left_low], axis=1),
+            jnp.concatenate([right_high, right_low, right_high], axis=1),
+            (((1,), (1,)), ((), ())), preferred_element_type=jnp.float32,
+        )
+
+    last = lambda x, y: field[PASSES, x, y, 0:groups].reshape(vectors, ez)
     images = []
     for x, y in every:
         k = number(x, y)
-        here = last(x, y)
+        here = field[PASSES, x, y, 0:groups]
         value = weight[6, k][None] * here
         for face in range(4):
             other = here if is_ghost(x, y, face) else here - beside(PASSES, x, y, face)
             value += weight[face, k][None] * other
         value += weight[4, k][None] * (here - pltpu.roll(here, ez - 1, 2))
         value += weight[5, k][None] * (here - pltpu.roll(here, 1, 2))
-        images.append(value)
+        images.append(value.reshape(vectors, ez))
     scale = 1.0 / (slope * math.sqrt(cells * ez))
     own = scale * product([last(x, y) for x, y in every], images)
     row = lax.broadcasted_iota(jnp.int32, own.shape, 0)
     column = lax.broadcasted_iota(jnp.int32, own.shape, 1)
     own += jnp.where(row == column, COARSE_SHIFT, 0.0)
+    own = jnp.concatenate([own, jnp.zeros((vectors, LANES - vectors), jnp.float32)], axis=1)
 
     for axis in range(3):
         receive(PASSES, axis)
-    x_face = product(
-        [last(ex, y) for y in range(1, ey + 1)],
-        [weight[0, number(ex, y)][None] * beside(PASSES, ex, y, 0) for y in range(1, ey + 1)],
-    )
-    y_face = product(
-        [last(x, ey) for x in range(1, ex + 1)],
-        [weight[2, number(x, ey)][None] * beside(PASSES, x, ey, 2) for x in range(1, ex + 1)],
-    )
-    z_face = product([zsend[PASSES, 0:groups]], [weight_z[...][None] * unpack(PASSES, groups)])
-    out_ref[iz, ix, iy] = jnp.concatenate(
-        [own, -scale * x_face, -scale * y_face, -scale * z_face], axis=1
-    )
+    zeros = jnp.zeros((vectors, ez), jnp.float32)
+
+    def placed(value, face):
+        rows = [zeros] * (LANES // vectors)
+        rows[face + 1] = value.reshape(vectors, ez)
+        return jnp.concatenate(rows, axis=0)
+
+    left, right = [], []
+    for y in range(1, ey + 1):
+        left.append(last(ex, y))
+        right.append(placed(weight[0, number(ex, y)][None] * beside(PASSES, ex, y, 0), 0))
+    for x in range(1, ex + 1):
+        left.append(last(x, ey))
+        right.append(placed(weight[2, number(x, ey)][None] * beside(PASSES, x, ey, 2), 1))
+    left.append(zsend[PASSES, 0:groups].reshape(vectors, ez))
+    right.append(placed(weight_z[...][None] * unpack(PASSES, groups), 2))
+    out_ref[iz, ix, iy] = own - scale * product(left, right)
 
     def spread(axis, index, count, source, sends, recvs, act):
         for step in range(1, count):
@@ -363,7 +373,7 @@
 
 def factor_kernel(
     counts, vectors, width, rows_local, cols_local,
-    slot_ref, blocks_ref, out_ref, place, strips, panel, local, across,
+    slot_hbm, blocks_ref, out_ref, slots, place, strips, panel, local, across, slot_sem,
 ):
     nx, ny, nz = counts
     ix, iy, iz = lax.axis_index("gx"), lax.axis_index("gy"), lax.axis_index("gz")
@@ -375,9 +385,17 @@
     own_cols = pl.ds(pl.multiple_of(iz * cols_local, LANES), cols_local)
     own_rows = pl.ds(pl.multiple_of(row_block * vectors, LANES), rows_local)
 
+    load = pltpu.make_async_copy(slot_hbm, slots, slot_sem)
+    load.start()
+
+    def slot_at(s):
+        return slots[s % nz, s // nz]
+
     def note(s, carry):
-        place[slot_ref[s]] = s
+        place[slot_at(s)] = s
         return carry
+
+    load.wait()
 
     lax.fori_loop(0, devices, note, 0, unroll=8)
     lane = lax.broadcasted_iota(jnp.int32, (vectors, LANES), 1)
@@ -405,9 +423,9 @@
         lower = []
         for face, (dr, dl, up, down) in enumerate(faces):
             n = jnp.where(up, s + dr * nz + dl, s)
-            put(jnp.where(up, slot_ref[n], devices), mine, (face + 1) * vectors)
+            put(jnp.where(up, slot_at(n), devices), mine, (face + 1) * vectors)
             n = jnp.where(down, s - dr * nz - dl, s)
-            lower.append(jnp.where(down, slot_ref[n], devices))
+            lower.append(jnp.where(down, slot_at(n), devices))
             r2, l2 = n // nz, n % nz
             below.append(pltpu.roll(blocks_ref[l2, r2 // ny, r2 % ny], LANES - (face + 1) * vectors, 1))
         turned = jnp.concatenate(below + [filler], axis=0).T[:vectors, :]
@@ -460,7 +478,7 @@
             ]
             for t in range(8):
                 head = columns[t][0][t : t + 1, :]
-                turn = 1.0 / head
+                turn = pl.reciprocal(head, approx=True)
                 pivot = jnp.where(row == t, head, pivot)
                 inverse = jnp.where(row == t, turn, inverse)
                 kept = [jnp.where(row > t, columns[t][0], 0.0)] + columns[t][1:]
@@ -516,8 +534,7 @@
     layers = layer_kappa.shape[0]
     groups = vectors // 8
     vmem = pl.BlockSpec(memory_space=pltpu.VMEM)
-    smem = pl.BlockSpec(memory_space=pltpu.SMEM)
-    anywhere = pl.BlockSpec(memory_space=pl.ANY)
+    anywhere = pl.BlockSpec(memory_space=pltpu.HBM)
     phases = PASSES + 1
     dma = pltpu.SemaphoreType.DMA
     blocks = pl.pallas_call(
@@ -539,7 +556,7 @@
             dma((ny,)), dma((ny,)), dma((nz, ny)), dma((nz, ny)), dma((nx, nz, ny)), dma((nx, nz, ny)),
         ],
         compiler_params=pltpu.CompilerParams(
-            collective_id=0, has_side_effects=True, vmem_limit_bytes=48 * 1024 * 1024
+            collective_id=0, has_side_effects=True, vmem_limit_bytes=(64 * 1024 - 640) * 1024
         ),
         name="basis",
     )(probe_vectors.reshape(vectors * ex * ey, ez), layer_ids, layer_kappa)
@@ -549,18 +566,20 @@
     return pl.pallas_call(
         functools.partial(factor_kernel, counts, vectors, width, rows_local, cols_local),
         out_shape=jax.ShapeDtypeStruct((rows_local, cols_local), jnp.float32),
-        in_specs=[smem, vmem],
+        in_specs=[anywhere, vmem],
         out_specs=vmem,
         scratch_shapes=[
+            pltpu.SMEM((nz, nx * ny), jnp.int32),
             pltpu.SMEM((nx * ny * nz,), jnp.int32),
             pltpu.VMEM((4, vectors, nx * ny * nz * vectors + LANES), jnp.float32),
             pltpu.VMEM((width, width + cols_local + rows_local), jnp.float32),
             pltpu.VMEM((rows_local, cols_local), jnp.float32),
             pltpu.VMEM((width, rows_local), jnp.float32),
+            dma(()),
         ],
         compiler_params=pltpu.CompilerParams(vmem_limit_bytes=48 * 1024 * 1024),
         name="factor",
-    )(slot_order.reshape(-1), blocks)
+    )(slot_order.T, blocks)
 
 
 def solution(mesh):

time: 46.5 us -> 46.6 us (level)
  Pallas kernels: 43.9 us -> 45.3 us
  local copies, waits for them, and re-layouts: 2.37 us -> 1.04 us
    unnamed x7 -> x4, local copies, waits for them, and re-layouts: 2.29 us -> 1.04 us
    pallas_call x1, Pallas kernels: 33.2 us -> 34.2 us  [on_device(): pl.pallas_call(functools.partial(basis_kernel, counts, (ex, ey, ez), vect...]
where the time goes in v4:
time: 46.6 us; the launch traced here: 46.4 us
  Pallas kernels  45.3 us (97%)
  local copies, waits for them, and re-layouts  1.04 us (2%)
    pallas_call x1, Pallas kernels, on_device(): pl.pallas_call(functools.partial(basis_kernel, counts, (ex, ey, ez), vect...  34.2 us
    pallas_call x1, Pallas kernels, on_device(): pl.pallas_call(functools.partial(factor_kernel, counts, vectors, width, r...  11.2 us
    unnamed x4, local copies, waits for them, and re-layouts  1.04 us

profile of v4, /device:TPU:0, one launch (start us, length us, event | category | flops | bytes accessed | tf_op | source)
XLA Modules:
  0.0 46.4 jit_solution(5607213102169155773)
XLA Ops:
  0.0 0.0 copy-start.1
  0.0 34.2 %basis.1.blocks_ref = f32[4,2,4,32,128]{4,3,2,1,0:T(8,128)} custom-call(f32[512,128]{1,0:T(8,128)} %bitcast.3, s32[2,8,128]{2,1,0:T(8,128)} %ids_hbm.1, f32[16]{0:T(128)} %kappa_hbm.1), custom_call_target="tpu_custom_call" | custom-call | tf_op jit(solution)/shard_map/basis/pallas_call | solution.py:540
  34.2 0.0 copy-done.1
  34.2 0.0 copy-start
  34.2 1.0 %copy-done = f32[4,2,4,32,128]{4,3,2,1,0:T(8,128)S(1)} copy-done((f32[4,2,4,32,128]{4,3,2,1,0:T(8,128)S(1)}, f32[4,2,4,32,128]{4,3,2,1,0:T(8,128)}, u32[]{:S(2)}) %copy-start) | copy-done | bytes 524312
  35.2 11.2 %factor.1 = f32[128,256]{1,0:T(8,128)} custom-call(s32[4,8]{1,0:T(4,128)S(1)} %bitcast.2, f32[4,2,4,32,128]{4,3,2,1,0:T(8,128)S(1)} %copy-done), custom_call_target="tpu_custom_call" | custom-call | tf_op jit(solution)/shard_map/factor/pallas_call | solution.py:566
Async XLA Ops:
  0.0 34.2 %copy-start.1 = (s32[8,4]{0,1:T(4,128)S(1)}, s32[8,4]{0,1:T(4,128)}, u32[]{:S(2)}) copy-start(s32[8,4]{0,1:T(4,128)} %param.7) | copy-start | bytes 388
  34.2 1.0 %copy-start = (f32[4,2,4,32,128]{4,3,2,1,0:T(8,128)S(1)}, f32[4,2,4,32,128]{4,3,2,1,0:T(8,128)}, u32[]{:S(2)}) copy-start(f32[4,2,4,32,128]{4,3,2,1,0:T(8,128)} %basis.1.blocks_ref) | copy-start | bytes 1572868

commit v5 on v4

--- a/solution.py
+++ b/solution.py
@@ -373,7 +373,7 @@
 
 def factor_kernel(
     counts, vectors, width, rows_local, cols_local,
-    slot_hbm, blocks_ref, out_ref, slots, place, strips, panel, local, across, slot_sem,
+    slot_hbm, blocks_ref, out_ref, slots, place, panel, local, across, slot_sem,
 ):
     nx, ny, nz = counts
     ix, iy, iz = lax.axis_index("gx"), lax.axis_index("gy"), lax.axis_index("gz")
@@ -382,11 +382,12 @@
     row_block = (ix * ny + iy) * (rows_local // vectors)
     wide = width // vectors
     per_tile = LANES // vectors
-    own_cols = pl.ds(pl.multiple_of(iz * cols_local, LANES), cols_local)
-    own_rows = pl.ds(pl.multiple_of(row_block * vectors, LANES), rows_local)
+    col_block = iz * (cols_local // vectors)
 
     load = pltpu.make_async_copy(slot_hbm, slots, slot_sem)
     load.start()
+    panel[...] = jnp.zeros(panel.shape, jnp.float32)
+    local[...] = jnp.zeros(local.shape, jnp.float32)
 
     def slot_at(s):
         return slots[s % nz, s // nz]
@@ -400,21 +401,29 @@
     lax.fori_loop(0, devices, note, 0, unroll=8)
     lane = lax.broadcasted_iota(jnp.int32, (vectors, LANES), 1)
     filler = jnp.zeros((LANES - 3 * vectors, LANES), jnp.float32)
-
-    def block_row(q, at):
-        strip = strips.at[at]
-        strip[...] = jnp.zeros(strip.shape, jnp.float32)
+    nowhere = 4 * devices
+    own_cols = (col_block, cols_local // vectors)
+    own_rows = (row_block, rows_local // vectors)
+
+    def block_row(q, ref, at, targets):
+        rows = pl.ds(pl.multiple_of(at * vectors, vectors), vectors)
         s = place[q]
         r, l = s // nz, s % nz
         i, j = r // ny, r % ny
 
         def put(c, value, lane_at):
-            cols = pl.ds(pl.multiple_of((c // per_tile) * LANES, LANES), LANES)
             begin = (c % per_tile) * vectors
             moved = pltpu.roll(value, lax.rem(begin + LANES - lane_at, LANES), 1)
-            pltpu.store(
-                strip.at[:, cols], moved, mask=(lane >= begin) & (lane < begin + vectors)
-            )
+            for (first, count), base in targets:
+                at_col = c - first
+                held = (at_col >= 0) & (at_col < count)
+                tile = jnp.clip(at_col, 0, count - 1) // per_tile
+                cols = pl.ds(pl.multiple_of(base + tile * LANES, LANES), LANES)
+                from_lane = jnp.where(held, begin, LANES)
+                pltpu.store(
+                    ref.at[rows, cols], moved,
+                    mask=(lane >= from_lane) & (lane < from_lane + vectors),
+                )
 
         mine = blocks_ref[l, i, j]
         put(q, mine, 0)
@@ -423,28 +432,23 @@
         lower = []
         for face, (dr, dl, up, down) in enumerate(faces):
             n = jnp.where(up, s + dr * nz + dl, s)
-            put(jnp.where(up, slot_at(n), devices), mine, (face + 1) * vectors)
+            put(jnp.where(up, slot_at(n), nowhere), mine, (face + 1) * vectors)
             n = jnp.where(down, s - dr * nz - dl, s)
-            lower.append(jnp.where(down, slot_at(n), devices))
+            lower.append(jnp.where(down, slot_at(n), nowhere))
             r2, l2 = n // nz, n % nz
             below.append(pltpu.roll(blocks_ref[l2, r2 // ny, r2 % ny], LANES - (face + 1) * vectors, 1))
         turned = jnp.concatenate(below + [filler], axis=0).T[:vectors, :]
         for face in range(3):
             put(lower[face], turned, face * vectors)
-        return strip
 
     def top_row(q, carry):
-        strip = block_row(q, q % 4)
-        rows = pl.ds(pl.multiple_of(q * vectors, vectors), vectors)
-        panel[rows, :width] = strip[:, :width]
-        panel[rows, width : width + cols_local] = strip[:, own_cols]
-        panel[rows, width + cols_local :] = strip[:, own_rows]
+        block_row(
+            q, panel, q, (((0, wide), 0), (own_cols, width), (own_rows, width + cols_local))
+        )
         return carry
 
     def own_row(n, carry):
-        strip = block_row(row_block + n, n % 4)
-        rows = pl.ds(pl.multiple_of(n * vectors, vectors), vectors)
-        local[rows, :] = strip[:, own_cols]
+        block_row(row_block + n, local, n, ((own_cols, 0),))
         return carry
 
     lax.fori_loop(0, wide, top_row, 0, unroll=4)
@@ -537,6 +541,7 @@
     anywhere = pl.BlockSpec(memory_space=pltpu.HBM)
     phases = PASSES + 1
     dma = pltpu.SemaphoreType.DMA
+    pinned = lambda value: pltpu.with_memory_space_constraint(value, pltpu.HBM)
     blocks = pl.pallas_call(
         functools.partial(basis_kernel, counts, (ex, ey, ez), vectors, layers),
         out_shape=jax.ShapeDtypeStruct((nz, nx, ny, vectors, LANES), jnp.float32),
@@ -556,10 +561,10 @@
             dma((ny,)), dma((ny,)), dma((nz, ny)), dma((nz, ny)), dma((nx, nz, ny)), dma((nx, nz, ny)),
         ],
         compiler_params=pltpu.CompilerParams(
-            collective_id=0, has_side_effects=True, vmem_limit_bytes=(64 * 1024 - 640) * 1024
+            collective_id=0, has_side_effects=True, vmem_limit_bytes=48 * 1024 * 1024
         ),
         name="basis",
-    )(probe_vectors.reshape(vectors * ex * ey, ez), layer_ids, layer_kappa)
+    )(pinned(probe_vectors.reshape(vectors * ex * ey, ez)), pinned(layer_ids), pinned(layer_kappa))
 
     rows_local, cols_local = nz * vectors, nx * ny * vectors
     width = NPAN * min(PANEL, rows_local, cols_local)
@@ -571,7 +576,6 @@
         scratch_shapes=[
             pltpu.SMEM((nz, nx * ny), jnp.int32),
             pltpu.SMEM((nx * ny * nz,), jnp.int32),
-            pltpu.VMEM((4, vectors, nx * ny * nz * vectors + LANES), jnp.float32),
             pltpu.VMEM((width, width + cols_local + rows_local), jnp.float32),
             pltpu.VMEM((rows_local, cols_local), jnp.float32),
             pltpu.VMEM((width, rows_local), jnp.float32),

time: 46.6 us -> 45.7 us (0.981)
  local copies, waits for them, and re-layouts: 1.04 us -> 0.01 us
    pallas_call x1, Pallas kernels: 11.2 us -> 12.2 us  [on_device(): pl.pallas_call(functools.partial(factor_kernel, counts, vectors, width, r...]
    unnamed x4 -> x2, local copies, waits for them, and re-layouts: 1.04 us -> 0.01 us
    pallas_call x1, Pallas kernels: 34.2 us -> 33.4 us  [on_device(): pl.pallas_call(functools.partial(basis_kernel, counts, (ex, ey, ez), vect...]
where the time goes in v5:
time: 45.7 us; the launch traced here: 45.6 us
  Pallas kernels  45.6 us (100%)
    pallas_call x1, Pallas kernels, on_device(): pl.pallas_call(functools.partial(basis_kernel, counts, (ex, ey, ez), vect...  33.4 us
    pallas_call x1, Pallas kernels, on_device(): pl.pallas_call(functools.partial(factor_kernel, counts, vectors, width, r...  12.2 us

profile of v5, /device:TPU:0, one launch (start us, length us, event | category | flops | bytes accessed | tf_op | source)
XLA Modules:
  0.0 45.6 jit_solution(350835127657064379)
XLA Ops:
  0.0 0.0 copy-start
  0.0 33.4 %basis.1.blocks_ref = f32[4,2,4,32,128]{4,3,2,1,0:T(8,128)S(1)} custom-call(f32[512,128]{1,0:T(8,128)} %bitcast.3, s32[2,8,128]{2,1,0:T(8,128)} %ids_hbm.1, f32[16]{0:T(128)} %kappa_hbm.1), custom_call_target="tpu_custom_call" | custom-call | tf_op jit(solution)/shard_map/basis/pallas_call | solution.py:545
  33.4 0.0 copy-done
  33.4 12.2 %factor.1 = f32[128,256]{1,0:T(8,128)} custom-call(s32[4,8]{1,0:T(4,128)S(1)} %bitcast.2, f32[4,2,4,32,128]{4,3,2,1,0:T(8,128)S(1)} %basis.1.blocks_ref), custom_call_target="tpu_custom_call" | custom-call | tf_op jit(solution)/shard_map/factor/pallas_call | solution.py:571
Async XLA Ops:
  0.0 33.4 %copy-start = (s32[8,4]{0,1:T(4,128)S(1)}, s32[8,4]{0,1:T(4,128)}, u32[]{:S(2)}) copy-start(s32[8,4]{0,1:T(4,128)} %param.7) | copy-start | bytes 388

commit v6 on v4

--- a/solution.py
+++ b/solution.py
@@ -373,7 +373,7 @@
 
 def factor_kernel(
     counts, vectors, width, rows_local, cols_local,
-    slot_hbm, blocks_ref, out_ref, slots, place, strips, panel, local, across, slot_sem,
+    slots, blocks_ref, out_ref, place, strips, panel, local, across,
 ):
     nx, ny, nz = counts
     ix, iy, iz = lax.axis_index("gx"), lax.axis_index("gy"), lax.axis_index("gz")
@@ -385,17 +385,12 @@
     own_cols = pl.ds(pl.multiple_of(iz * cols_local, LANES), cols_local)
     own_rows = pl.ds(pl.multiple_of(row_block * vectors, LANES), rows_local)
 
-    load = pltpu.make_async_copy(slot_hbm, slots, slot_sem)
-    load.start()
-
     def slot_at(s):
         return slots[s % nz, s // nz]
 
     def note(s, carry):
         place[slot_at(s)] = s
         return carry
-
-    load.wait()
 
     lax.fori_loop(0, devices, note, 0, unroll=8)
     lane = lax.broadcasted_iota(jnp.int32, (vectors, LANES), 1)
@@ -537,6 +532,7 @@
     anywhere = pl.BlockSpec(memory_space=pltpu.HBM)
     phases = PASSES + 1
     dma = pltpu.SemaphoreType.DMA
+    pinned = lambda value: pltpu.with_memory_space_constraint(value, pltpu.HBM)
     blocks = pl.pallas_call(
         functools.partial(basis_kernel, counts, (ex, ey, ez), vectors, layers),
         out_shape=jax.ShapeDtypeStruct((nz, nx, ny, vectors, LANES), jnp.float32),
@@ -556,26 +552,24 @@
             dma((ny,)), dma((ny,)), dma((nz, ny)), dma((nz, ny)), dma((nx, nz, ny)), dma((nx, nz, ny)),
         ],
         compiler_params=pltpu.CompilerParams(
-            collective_id=0, has_side_effects=True, vmem_limit_bytes=(64 * 1024 - 640) * 1024
+            collective_id=0, has_side_effects=True, vmem_limit_bytes=48 * 1024 * 1024
         ),
         name="basis",
-    )(probe_vectors.reshape(vectors * ex * ey, ez), layer_ids, layer_kappa)
+    )(pinned(probe_vectors.reshape(vectors * ex * ey, ez)), pinned(layer_ids), pinned(layer_kappa))
 
     rows_local, cols_local = nz * vectors, nx * ny * vectors
     width = NPAN * min(PANEL, rows_local, cols_local)
     return pl.pallas_call(
         functools.partial(factor_kernel, counts, vectors, width, rows_local, cols_local),
         out_shape=jax.ShapeDtypeStruct((rows_local, cols_local), jnp.float32),
-        in_specs=[anywhere, vmem],
+        in_specs=[pl.BlockSpec(memory_space=pltpu.SMEM), vmem],
         out_specs=vmem,
         scratch_shapes=[
-            pltpu.SMEM((nz, nx * ny), jnp.int32),
             pltpu.SMEM((nx * ny * nz,), jnp.int32),
             pltpu.VMEM((4, vectors, nx * ny * nz * vectors + LANES), jnp.float32),
             pltpu.VMEM((width, width + cols_local + rows_local), jnp.float32),
             pltpu.VMEM((rows_local, cols_local), jnp.float32),
             pltpu.VMEM((width, rows_local), jnp.float32),
-            dma(()),
         ],
         compiler_params=pltpu.CompilerParams(vmem_limit_bytes=48 * 1024 * 1024),
         name="factor",

time: 46.6 us -> 44.7 us (0.959)
  local copies, waits for them, and re-layouts: 1.04 us -> 0.01 us
  Pallas kernels: 45.3 us -> 44.5 us
    unnamed x4 -> x2, local copies, waits for them, and re-layouts: 1.04 us -> 0.01 us
    pallas_call x1, Pallas kernels: 34.2 us -> 33.4 us  [on_device(): pl.pallas_call(functools.partial(basis_kernel, counts, (ex, ey, ez), vect...]
where the time goes in v6:
time: 44.7 us; the launch traced here: 44.6 us
  Pallas kernels  44.5 us (100%)
    pallas_call x1, Pallas kernels, on_device(): pl.pallas_call(functools.partial(basis_kernel, counts, (ex, ey, ez), vect...  33.4 us
    pallas_call x1, Pallas kernels, on_device(): pl.pallas_call(functools.partial(factor_kernel, counts, vectors, width, r...  11.2 us

profile of v6, /device:TPU:0, one launch (start us, length us, event | category | flops | bytes accessed | tf_op | source)
XLA Modules:
  0.0 44.6 jit_solution(17860209477361401433)
XLA Ops:
  0.0 0.0 copy-start
  0.0 33.4 %basis.1.blocks_ref = f32[4,2,4,32,128]{4,3,2,1,0:T(8,128)S(1)} custom-call(f32[512,128]{1,0:T(8,128)} %bitcast.3, s32[2,8,128]{2,1,0:T(8,128)} %ids_hbm.1, f32[16]{0:T(128)} %kappa_hbm.1), custom_call_target="tpu_custom_call" | custom-call | tf_op jit(solution)/shard_map/basis/pallas_call | solution.py:536
  33.4 0.0 copy-done
  33.4 11.2 %factor.1 = f32[128,256]{1,0:T(8,128)} custom-call(s32[4,8]{1,0:T(4,128)S(1)} %bitcast.2, f32[4,2,4,32,128]{4,3,2,1,0:T(8,128)S(1)} %basis.1.blocks_ref), custom_call_target="tpu_custom_call" | custom-call | tf_op jit(solution)/shard_map/factor/pallas_call | solution.py:562
Async XLA Ops:
  0.0 33.4 %copy-start = (s32[8,4]{0,1:T(4,128)S(1)}, s32[8,4]{0,1:T(4,128)}, u32[]{:S(2)}) copy-start(s32[8,4]{0,1:T(4,128)} %param.7) | copy-start | bytes 388
